TPU v7x, 128 devices: a whole 4x4x4 slice. The times are simulated.
128 devices in a mesh: dp: 8 (over z, core), owner: 16 (over y, x).
Axes of the slice: x: 4, y: 4, z: 4, core: 2. Of those that a mesh axis runs over, the one named last changes fastest.
Arguments:
- partials: bfloat16 [8, 64, 1024, 1024], P('dp', None, 'owner'), may hold values from -6 to 6
- owner_blocks: int32 [128, 2], replicated, may hold values from -1 to 63, as said below
- left_root: bfloat16 [128, 2, 1024, 1024], P(('dp', 'owner')), may hold values from -1 to 4
- right_root: bfloat16 [128, 2, 1024, 1024], P(('dp', 'owner')), may hold values from -1 to 4
Outputs:
- left_stat: bfloat16 [128, 2, 1024, 1024], P(('dp', 'owner'))
- right_stat: bfloat16 [128, 2, 1024, 1024], P(('dp', 'owner'))
- update: bfloat16 [64, 1024, 1024], P(None, 'owner', 'dp')
Inputs may be any that keep to these rules, and one draw needn't show every extreme that they name: `owner_blocks`: every block number 0 to 63 stands in exactly one slot, and -1 marks an empty slot. The owners of data group d are rows d times the owner count onward, one row per owner; their slots hold exactly 8 blocks together. An owner holds 0 to 2 blocks, and in every data group some owner holds 2.
All inputs are finite; a program needn't handle non-finite values.
Results may differ from a plain program's by a relative error of at most 0.02.
Values may be sent and summed in bfloat16 or wider, within the bound.
No kernel may reach another device: no remote copies, remote signals or barrier semaphores. Data moves between devices by JAX's collectives and lax.ppermute only.
A program may use at most 128 MiB of HBM per device.

v0:
```python
import jax
import jax.numpy as jnp
from jax import lax
from jax.sharding import PartitionSpec as P


def slot_products(grad_bf, left_inv, right_inv):
    blocksize = grad_bf.shape[-1]
    left_stat = jnp.dot(grad_bf, grad_bf.T, preferred_element_type=jnp.float32) / blocksize
    right_stat = jnp.dot(grad_bf.T, grad_bf, preferred_element_type=jnp.float32) / blocksize
    left_half = jnp.dot(left_inv, grad_bf, preferred_element_type=jnp.float32).astype(jnp.bfloat16)
    updated = jnp.dot(left_half, right_inv, preferred_element_type=jnp.float32)
    return (
        left_stat.astype(jnp.bfloat16),
        right_stat.astype(jnp.bfloat16),
        updated.astype(jnp.bfloat16),
    )


def local(partials, owner_blocks, left_root, right_root):
    replicas = lax.axis_size("dp")
    owners = lax.axis_size("owner")
    group_id = lax.axis_index("dp")
    local_part = partials[0]
    nblocks, row_part, blocksize = local_part.shape
    slot_count = owner_blocks.shape[1]
    slot_list = owner_blocks.reshape(-1)
    is_live = slot_list >= 0
    live_rank = jnp.cumsum(is_live.astype(jnp.int32)) - 1
    block_order = (
        jnp.zeros((nblocks,), jnp.int32)
        .at[jnp.where(is_live, live_rank, nblocks)]
        .set(slot_list, mode="drop")
    )
    slot_of_block = (
        jnp.zeros((nblocks,), jnp.int32)
        .at[jnp.where(is_live, slot_list, nblocks)]
        .set(jnp.arange(slot_list.shape[0], dtype=jnp.int32), mode="drop")
    )
    sorted_parts = jnp.take(local_part, block_order, axis=0)
    group_sums = lax.psum_scatter(sorted_parts, "dp", scatter_dimension=0, tiled=True).astype(
        jnp.float32
    )
    group_list = lax.dynamic_slice_in_dim(
        slot_list, group_id * owners * slot_count, owners * slot_count, 0
    )
    group_live = group_list >= 0
    group_rank = jnp.cumsum(group_live.astype(jnp.int32)) - 1
    pick_index = jnp.maximum(group_rank, 0).reshape(owners, slot_count).T.reshape(-1)
    pick_live = group_live.reshape(owners, slot_count).T.reshape(-1)
    taken = jnp.take(group_sums, pick_index, axis=0)
    outgoing = jnp.where(pick_live[:, None, None], taken, 0.0).astype(jnp.bfloat16)
    outgoing = outgoing.reshape(slot_count, owners, row_part, blocksize)
    arrived = lax.all_to_all(outgoing, "owner", split_axis=1, concat_axis=1, tiled=True)
    gradient = arrived.reshape(slot_count, owners * row_part, blocksize)
    left_list = []
    right_list = []
    update_list = []
    for slot_idx in range(slot_count):
        grad_bf = gradient[slot_idx]
        left_inv = left_root[0, slot_idx]
        right_inv = right_root[0, slot_idx]
        left_stat, right_stat, updated = slot_products(grad_bf, left_inv, right_inv)
        left_list.append(left_stat)
        right_list.append(right_stat)
        update_list.append(updated)
    left_out = jnp.stack(left_list)[None]
    right_out = jnp.stack(right_list)[None]
    all_updates = jnp.stack(update_list)
    col_part = blocksize // replicas
    pieces = all_updates.reshape(slot_count, owners, row_part, replicas, col_part).transpose(
        3, 1, 0, 2, 4
    )
    received = lax.all_to_all(
        pieces.reshape(replicas * owners, slot_count, row_part, col_part),
        ("dp", "owner"),
        split_axis=0,
        concat_axis=0,
        tiled=True,
    )
    received = received.reshape(replicas * owners * slot_count, row_part, col_part)
    update = jnp.take(received, slot_of_block, axis=0)
    return (left_out, right_out, update)


def solution(mesh):
    in_specs = (
        P("dp", None, "owner", None),
        P(),
        P(("dp", "owner"), None, None, None),
        P(("dp", "owner"), None, None, None),
    )
    out_specs = (
        P(("dp", "owner"), None, None, None),
        P(("dp", "owner"), None, None, None),
        P(None, "owner", "dp"),
    )
    return jax.shard_map(local, mesh=mesh, in_specs=in_specs, out_specs=out_specs, check_vma=False)
```

profile of v0, /device:TPU:1, one launch (start us, length us, event | category | flops | bytes accessed | tf_op | source)
XLA Modules:
  0.0 245.0 jit_solution(4984032784027878726)
XLA Ops:
  7.2 0.0 reduce-scatter.2.cloned.1.call-start
  7.2 0.7 compare_convert_fusion
  7.9 0.8 copy.38
  8.7 0.1 reshape.189
  8.8 0.1 reshape.226
  9.0 0.1 copy.43
  9.1 0.1 reshape.197
  9.2 0.3 reduce-window.14
  9.5 0.1 slice.27
  9.6 0.1 slice_reduce_fusion
  9.8 0.1 add_add_fusion
  9.8 1.4 scatter_custom_fusion
  11.3 8.9 %gather_fusion = bf16[64,64,1024]{2,1,0:T(8,128)(2,1)} fusion(bf16[64,64,1024]{2,1,0:T(8,128)(2,1)} %bitcast.96, s32[1024]{0:T(1024)S(1)} %pad_clamp_fusion.2), kind=kCustom, calls=%fused_computation | custom fusion | bytes 16777472 | tf_op jit(solution)/shard_map/jit(_take)/gather | solution.py:40
  20.2 7.5 %broadcast_select_fusion = bf16[64,64,1024]{2,1,0:T(8,128)(2,1)} fusion(bf16[64,64,1024]{2,1,0:T(8,128)(2,1)} %gather_fusion, pred[64]{0:T(512)(128)(4,1)S(1)} %compare_and_fusion.2), kind=kLoop, calls=%fused_computation.6 | loop fusion | flops 4194304 | bytes 16777280 | tf_op jit(solution)/shard_map/jit(_take)/select_n | solution.py:40
  27.7 0.0 reduce-scatter.2.cloned.1.call-update
  27.7 0.1 convert_bitcast_fusion.2
  27.8 0.1 copy.40
  27.9 0.1 reduce-window.11
  27.9 0.1 maximum_reduce_fusion
  28.0 0.1 max.8
  28.1 0.1 copy.44
  28.2 0.1 reshape.242
  28.3 0.1 copy.41
  28.4 0.1 reshape.187
  28.5 0.1 copy.39
  28.6 0.1 fusion.42
  28.8 54.3 %reduce-scatter.2.cloned.1.call-done = bf16[8,64,1024]{2,1,0:T(8,128)(2,1)} async-done(((bf16[64,64,1024]{2,1,0:T(8,128)(2,1)}), bf16[8,64,1024]{2,1,0:T(8,128)(2,1)}) %reduce-scatter.2.cloned.1.call-update) | async-done | bytes 1048592 | tf_op jit(solution)/shard_map/reduce_scatter | solution.py:41
  83.1 4.1 %gather_fusion.1 = bf16[32,64,1024]{2,1,0:T(8,128)(2,1)} fusion(bf16[8,64,1024]{2,1,0:T(8,128)(2,1)} %reduce-scatter.2.cloned.1.call-done, s32[1024]{0:T(1024)S(1)} %pad_clamp_fusion.1), kind=kCustom, calls=%fused_computation.1 | custom fusion | bytes 8388736 | tf_op jit(solution)/shard_map/jit(_take)/gather | solution.py:51
  87.1 4.3 %select_convert_fusion = bf16[2,16,64,1024]{3,2,1,0:T(8,128)(2,1)S(1)} fusion(bf16[2,16,64,1024]{3,2,1,0:T(8,128)(2,1)} %bitcast.95, pred[2,16]{1,0:T(4,128)(4,1)S(1)} %copy.41, pred[2,16]{1,0:T(4,128)(4,1)S(1)} %copy.39), kind=kLoop, calls=%fused_computation.5 | loop fusion | flops 4194304 | bytes 8388672 | tf_op jit(solution)/shard_map/convert_element_type | solution.py:52
  91.4 0.7 copy.48
  92.1 56.1 %all_to_all.10 = bf16[2,16,64,1024]{3,2,0,1:T(8,128)(2,1)S(1)} all-to-all(bf16[2,16,64,1024]{3,2,0,1:T(8,128)(2,1)S(1)} %copy.48), channel_id=1, replica_groups=mesh['dp'=8,'owner'=16] {'owner'}, dimensions={1} | all-to-all | bytes 8388608 | tf_op jit(solution)/shard_map/all_to_all | solution.py:54
  148.2 0.0 copy-start
  148.2 2.9 %fusion.49 = (bf16[1,16,64,1024]{3,2,0,1:T(8,128)(2,1)}, bf16[1,16,64,1024]{3,2,0,1:T(8,128)(2,1)}) fusion(bf16[2,16,64,1024]{3,2,0,1:T(8,128)(2,1)S(1)} %all_to_all.10), kind=kLoop, calls=%fused_computation.66 | loop fusion | bytes 8388608 | tf_op jit(solution)/shard_map/slice | solution.py:60
  151.2 0.6 copy-done
  151.8 7.4 %convert_bitcast_fusion.1 = bf16[128,8,8,128]{3,1,2,0:T(8,128)(2,1)S(1)} fusion(bf16[1,2,1024,1024]{3,2,1,0:T(8,128)(2,1)} %param.7, bf16[1024,1024]{1,0:T(8,128)(2,1)} %bitcast.101, bf16[1,2,1024,1024]{3,2,1,0:T(8,128)(2,1)} %param.6), kind=kOutput, calls=%fused_computation.30 | convolution fusion | flops 4297064448 | bytes 8388608 | tf_op jit(solution)/shard_map/dot_general | solution.py:12
  159.2 0.6 copy.55
  159.9 0.5 copy.51
  160.4 8.8 %convert_bitcast_fusion = bf16[128,8,8,128]{3,1,2,0:T(8,128)(2,1)} fusion(bf16[1,2,1024,1024]{3,2,1,0:T(8,128)(2,1)} %param.7, bf16[1024,1024]{1,0:T(8,128)(2,1)} %bitcast.99, bf16[1,2,1024,1024]{3,2,1,0:T(8,128)(2,1)} %param.6), kind=kOutput, calls=%fused_computation.26 | convolution fusion | flops 4297064448 | bytes 8388608 | tf_op jit(solution)/shard_map/dot_general | solution.py:12
  169.2 2.2 copy.56
  171.4 0.5 copy.52
  172.0 2.4 pad_maximum_fusion
  174.4 0.0 copy-start.3
  174.4 8.1 %all-to-all-start.1 = ((bf16[128,2,64,128]{3,2,1,0:T(8,128)(2,1)}), bf16[128,2,64,128]{3,2,1,0:T(8,128)(2,1)}, u32[]{:S(2)}, u32[]{:S(2)}) async-start(bf16[128,2,64,128]{3,2,1,0:T(8,128)(2,1)} %bitcast.94), calls=%async_computation.2 | async-start | bytes 8388608 | tf_op jit(solution)/shard_map/all_to_all | solution.py:74
  182.5 1.4 scatter_custom_fusion.1
  184.0 0.0 copy-done.3
  184.0 0.0 copy-start.2
  184.0 2.4 fusion.26
  186.4 0.0 copy-done.2
  186.4 0.0 copy-start.1
  186.4 2.4 fusion.27
  188.8 0.0 copy-done.1
  188.8 2.4 fusion.28
  191.2 2.4 fusion.31
  193.6 3.7 %maximum_bitcast_fusion = (bf16[1,2,1024,1024]{3,2,1,0:T(8,128)(2,1)}, bf16[1,2,1024,1024]{3,2,1,0:T(8,128)(2,1)}) fusion(bf16[1,1024,1024]{2,1,0:T(8,128)(2,1)S(1)} %fusion.27, bf16[1,1024,1024]{2,1,0:T(8,128)(2,1)S(1)} %fusion.26, bf16[1,1024,1024]{2,1,0:T(8,128)(2,1)S(1)} %fusion.31, bf16[1,1024,1024]{2,1,0:T(8,128)(2,1)S(1)} %fusion.28), kind=kLoop, calls=%fused_computation.7 | loop fusion | flops 4194304 | bytes 16777216 | tf_op jit(solution)/shard_map/broadcast_in_dim | solution.py:67
  197.3 36.7 %all-to-all-done.1 = bf16[128,2,64,128]{3,2,1,0:T(8,128)(2,1)} async-done(((bf16[128,2,64,128]{3,2,1,0:T(8,128)(2,1)}), bf16[128,2,64,128]{3,2,1,0:T(8,128)(2,1)}, u32[]{:S(2)}, u32[]{:S(2)}) %all-to-all-start.1) | async-done | bytes 4194336 | tf_op jit(solution)/shard_map/all_to_all | solution.py:74
  234.0 2.9 %gather_fusion.2 = bf16[64,64,128]{2,1,0:T(8,128)(2,1)S(1)} fusion(bf16[256,64,128]{2,1,0:T(8,128)(2,1)} %bitcast.26, s32[1024]{0:T(1024)S(1)} %pad_clamp_fusion), kind=kCustom, calls=%fused_computation.2 | custom fusion | bytes 2097408 | tf_op jit(solution)/shard_map/jit(_take)/gather | solution.py:82
  237.0 1.1 broadcast_select_fusion.1
  (11 shorter events, 0.1 us)
Async XLA Ops:
  7.2 75.9 %reduce-scatter.2.cloned.1.call-start = ((), (), s32[]{:S(2)}) async-start(), calls=%async_computation.3 | async-start | bytes 9437184 | tf_op jit(solution)/shard_map/reduce_scatter | solution.py:41
  148.2 3.5 %copy-start = (bf16[2,16,64,1024]{3,2,0,1:T(8,128)(2,1)}, bf16[2,16,64,1024]{3,2,0,1:T(8,128)(2,1)S(1)}, u32[]{:S(2)}) copy-start(bf16[2,16,64,1024]{3,2,0,1:T(8,128)(2,1)S(1)} %all_to_all.10) | copy-start | bytes 12582916
  174.4 9.6 %copy-start.3 = (bf16[1,16,64,1024]{3,2,0,1:T(8,128)(2,1)S(1)}, bf16[1,16,64,1024]{3,2,0,1:T(8,128)(2,1)}, u32[]{:S(2)}) copy-start(bf16[1,16,64,1024]{3,2,0,1:T(8,128)(2,1)} %get-tuple-element.5) | copy-start | bytes 6291460
  174.4 59.7 %all-to-all-start.1 = ((bf16[128,2,64,128]{3,2,1,0:T(8,128)(2,1)}), bf16[128,2,64,128]{3,2,1,0:T(8,128)(2,1)}, u32[]{:S(2)}, u32[]{:S(2)}) async-start(bf16[128,2,64,128]{3,2,1,0:T(8,128)(2,1)} %bitcast.94), calls=%async_computation.2 | async-start | bytes 8388608 | tf_op jit(solution)/shard_map/all_to_all | solution.py:74
  184.0 2.4 copy-start.2
  186.4 2.4 copy-start.1
Sparse Core Ops, SparseCore 0:
  27.8 55.1 reduce-scatter.1
where the time goes:
time: 245 us
  waiting for transfers between devices  91 us (37%)
  blocking collectives  56.1 us (23%)
  local copies, waits for them, and re-layouts  29 us (12%)
  matrix products  25.8 us (11%)
  other arithmetic  20.5 us (8%)
  between operations  14.3 us (6%)
  starting transfers between devices  8.18 us (3%)
    all_to_all x1, blocking collectives, local(): lax.all_to_all(outgoing, 'owner', split_axis=1, concat_axis=1, tiled=True)  56.1 us
    reduce_scatter x1, waiting for transfers between devices, local(): lax.psum_scatter(sorted_parts, 'dp', scatter_dimension=0, tiled=True)  54.3 us
    all_to_all x1, waiting for transfers between devices, local(): lax.all_to_all(pieces.reshape(replicas * owners, slot_count, row_part, co...  36.7 us
    dot_general x2, matrix products, slot_products(): updated = jnp.dot(left_half, right_inv, preferred_element_type=jnp.float32)  16.2 us
    gather x1, local copies, waits for them, and re-layouts, local(): sorted_parts = jnp.take(local_part, block_order, axis=0)  8.92 us
    all_to_all x1, starting transfers between devices, local(): lax.all_to_all(pieces.reshape(replicas * owners, slot_count, row_part, co...  8.14 us
    select_n x2, other arithmetic, local(): sorted_parts = jnp.take(local_part, block_order, axis=0)  7.48 us
  transfers between devices with their start and end apart: 2, of which 2 were waited for; matrix products, arithmetic and copies ran while one was open for 6% of the time, Pallas kernels for 0%

commit v1 on v0

v1 whole, which is shorter than its diff:
```python
import jax
import jax.numpy as jnp
from jax import lax
from jax.experimental import pallas as pl
from jax.experimental.pallas import tpu as pltpu
from jax.sharding import Mesh, PartitionSpec as P

SPLITS = (256, 256, 512)
GROUPS = 8
NBLOCKS = 64
F32 = jnp.float32
BF16 = jnp.bfloat16
VMEM = pl.BlockSpec(memory_space=pltpu.VMEM)
SMEM = pl.BlockSpec(memory_space=pltpu.SMEM)
HBM = pl.BlockSpec(memory_space=pltpu.HBM)


def params(mebibytes):
    return pltpu.CompilerParams(vmem_limit_bytes=mebibytes * 1024 * 1024)


def cost(flops, nbytes):
    return pl.CostEstimate(flops=flops, bytes_accessed=nbytes, transcendentals=0)


def shape(*dims):
    return jax.ShapeDtypeStruct(dims, BF16)


def add(*terms):
    total = terms[0].astype(F32)
    for term in terms[1:]:
        total = total + term.astype(F32)
    return total.astype(BF16)


def wanted(core):
    low, high = range(4), range(4, 8)
    z = lax.axis_index("z")
    places = []
    for shift, ranks in ((2, low), (1, high), (2, high), (3, low), (1, low), (3, high), (0, low), (0, high)):
        group = lax.rem(z + shift, 4) * 2 + core
        places += [group * 9 + rank for rank in ranks]
    return places


def block_table(owner_blocks, blocks):
    rank = [jnp.int32(0)] * GROUPS
    for slot in range(32):
        for g in range(GROUPS):
            block = owner_blocks[slot % 2, g * 16 + slot // 2]
            blocks[g * 9 + rank[g]] = block
            rank[g] = rank[g] + (block >= 0).astype(jnp.int32)


def copy_blocks(blocks, core, part_ref, outs, sems):
    numbers = [blocks[place] for place in wanted(core)]
    first = 0
    copies = []
    for k, out in enumerate(outs):
        columns = pl.ds(first, out.shape[-1])
        for j, block in enumerate(numbers):
            pltpu.make_async_copy(part_ref.at[block, :, columns], out.at[j], sems.at[k]).start()
        copies.append(pltpu.make_async_copy(part_ref.at[pl.ds(0, 32), :, columns], out, sems.at[k]))
        first += out.shape[-1]
    for copy in copies:
        copy.wait()


def gather_partner(owner_blocks, partials):
    rows, size = partials.shape[1:]

    def body(table_ref, part_ref, blocks, *refs):
        block_table(table_ref, blocks)
        copy_blocks(blocks, 1 - lax.axis_index("core"), part_ref, refs[:-1], refs[-1])

    return pl.pallas_call(
        body,
        in_specs=[SMEM, HBM],
        out_specs=[SMEM, VMEM, VMEM],
        out_shape=[jax.ShapeDtypeStruct((GROUPS * 9,), jnp.int32)]
        + [shape(32, rows, w) for w in (SPLITS[0], size - SPLITS[0])],
        scratch_shapes=[pltpu.SemaphoreType.DMA((2,))],
        compiler_params=params(48),
        cost_estimate=cost(0, 2 * 32 * rows * size * 2),
        name="gather_partner",
    )(owner_blocks, partials)


def gather_own(blocks, partials):
    rows, size = partials.shape[1:]

    def body(block_ref, part_ref, *refs):
        copy_blocks(block_ref, lax.axis_index("core"), part_ref, refs[:-1], refs[-1])

    return pl.pallas_call(
        body,
        in_specs=[SMEM, HBM],
        out_specs=[VMEM] * len(SPLITS),
        out_shape=[shape(32, rows, w) for w in SPLITS],
        scratch_shapes=[pltpu.SemaphoreType.DMA((len(SPLITS),))],
        compiler_params=params(44),
        cost_estimate=cost(0, 2 * 32 * rows * size * 2),
        name="gather_own",
    )(blocks, partials)


def add_pair(own, received, first):
    _, rows, width = own.shape

    def body(own_ref, got_ref, *outs):
        for which, out in enumerate(outs):
            for t in range(8):
                j = 8 * which + t
                out[t] = add(own_ref[j], got_ref[j, :, first : first + width])

    return pl.pallas_call(
        body,
        in_specs=[VMEM, VMEM],
        out_specs=[VMEM] * 4,
        out_shape=[shape(8, rows, width)] * 4,
        compiler_params=params(16),
        cost_estimate=cost(0, 3 * 32 * rows * width * 2),
        name="add_core_pair",
    )(own, received)


def add_waiting(waiting, got_up, got_down):
    _, rows, width = waiting.shape

    def body(wait_ref, up_ref, down_ref, up_out, down_out):
        for t in range(4):
            up_out[t] = add(wait_ref[t], up_ref[t])
            down_out[t] = add(wait_ref[4 + t], down_ref[t])

    return pl.pallas_call(
        body,
        in_specs=[VMEM] * 3,
        out_specs=[VMEM] * 2,
        out_shape=[shape(4, rows, width)] * 2,
        compiler_params=params(16),
        cost_estimate=cost(0, 24 * rows * width * 2),
        name="add_waiting",
    )(waiting, got_up, got_down)


def add_last_and_pick(owner_blocks, chunks):
    rows = chunks[0][0].shape[1]
    widths = [chunk[0].shape[2] for chunk in chunks]

    def body(table_ref, *refs):
        ins, (out_ref, total, sem) = refs[:-3], refs[-3:]
        first = 0
        for k, width in enumerate(widths):
            own_ref, up_ref, down_ref, late_up_ref, late_down_ref = ins[5 * k : 5 * k + 5]
            columns = slice(first, first + width)
            for t in range(4):
                total[t, :, columns] = add(own_ref[t], late_up_ref[t], down_ref[4 + t])
                total[4 + t, :, columns] = add(own_ref[4 + t], late_down_ref[t], up_ref[4 + t])
            first += width
        start = (lax.axis_index("z") * 2 + lax.axis_index("core")) * 16
        rank = jnp.int32(0)
        for slot in range(32):
            pltpu.make_async_copy(
                total.at[jnp.minimum(rank, 7)], out_ref.at[slot // 2, slot % 2], sem
            ).start()
            rank = rank + (table_ref[slot % 2, start + slot // 2] >= 0).astype(jnp.int32)
        pltpu.make_async_copy(out_ref, out_ref, sem).wait()

    return pl.pallas_call(
        body,
        in_specs=[SMEM] + [VMEM] * (5 * len(chunks)),
        out_specs=HBM,
        out_shape=shape(16, 2, rows, sum(widths)),
        scratch_shapes=[pltpu.VMEM((8, rows, sum(widths)), BF16), pltpu.SemaphoreType.DMA],
        compiler_params=params(16),
        cost_estimate=cost(0, 56 * rows * sum(widths) * 2),
        name="add_last_and_pick",
    )(owner_blocks, *[array for chunk in chunks for array in chunk])


def left_product(left_root, arrived):
    owners, slots, rows, width = arrived.shape
    size = owners * rows

    def body(left_ref, grad_ref, out_ref):
        grad = grad_ref[:, 0].reshape(size, width)
        out_ref[0] = jnp.dot(left_ref[0], grad, preferred_element_type=F32).astype(BF16)

    return pl.pallas_call(
        body,
        grid=(slots,),
        in_specs=[
            pl.BlockSpec((1, size, size), lambda c: (c, 0, 0)),
            pl.BlockSpec((owners, 1, rows, width), lambda c: (0, c, 0, 0)),
        ],
        out_specs=pl.BlockSpec((1, size, width), lambda c: (c, 0, 0)),
        out_shape=shape(slots, size, width),
        compiler_params=params(24),
        cost_estimate=cost(2 * slots * size * size * width, 2 * slots * size * (size + 2 * width)),
        name="left_product",
    )(left_root, arrived)


def finish_update(left_root, right_root, left_part, arrived):
    owners, slots, rows, width = arrived.shape
    size = owners * rows
    done = size - width
    tile, col = 256, 128
    cuts = [(at, min(tile, width - at)) for at in range(0, width, tile)]
    per = tile // col

    def body(left_ref, right_ref, part_ref, grad_ref, out_ref, left, right, part, grad, half, out, sems, out_sem):
        copies = {}

        def fetch(name, source, target):
            copies[name] = pltpu.make_async_copy(source, target, sems.at[len(copies)])
            copies[name].start()

        for c in range(slots):
            fetch((c, "left"), left_ref.at[c], left.at[c])
            fetch((c, "grad"), grad_ref.at[:, c], grad.at[c])
            fetch((c, "part"), part_ref.at[c], part.at[c])
            fetch((c, "right"), right_ref.at[c], right.at[c])
        for c in range(slots):
            for name in ("left", "grad"):
                copies[c, name].wait()
            for n, (at, wide) in enumerate(cuts):
                half[:, done + at : done + at + wide] = jnp.dot(
                    left[c], grad[c, :, :, at : at + wide].reshape(size, wide), preferred_element_type=F32
                ).astype(BF16)
            for name in ("part", "right"):
                copies[c, name].wait()
            half[:, :done] = part[c]
            for n in range(size // tile):
                total = jnp.dot(
                    half[...], right[c, :, n * tile : (n + 1) * tile], preferred_element_type=F32
                ).astype(BF16)
                for t in range(per):
                    out[n * per + t, :, c] = total[:, t * col : (t + 1) * col].reshape(owners, rows, col)
                pieces = pl.ds(n * per, per)
                pltpu.make_async_copy(out.at[pieces, :, c], out_ref.at[pieces, :, c], out_sem).start()
        pltpu.make_async_copy(out, out_ref, out_sem).wait()

    return pl.pallas_call(
        body,
        in_specs=[HBM] * 4,
        out_specs=HBM,
        out_shape=shape(size // col, owners, slots, rows, col),
        scratch_shapes=[
            pltpu.VMEM((slots, size, size), BF16),
            pltpu.VMEM((slots, size, size), BF16),
            pltpu.VMEM((slots, size, done), BF16),
            pltpu.VMEM((slots, owners, rows, width), BF16),
            pltpu.VMEM((size, size), BF16),
            pltpu.VMEM((size // col, owners, slots, rows, col), BF16),
            pltpu.SemaphoreType.DMA((4 * slots,)),
            pltpu.SemaphoreType.DMA,
        ],
        compiler_params=params(59),
        cost_estimate=cost(2 * slots * size * size * (width + size), 6 * slots * size * size),
        name="finish_update",
    )(left_root, right_root, left_part, arrived)


def gram_products(owner_blocks, arrived):
    owners, slots, rows, _ = arrived[0].shape
    size = owners * rows
    tile = 256
    count = len(arrived)

    def body(table_ref, *refs):
        parts, (left_out, right_out, places, grad) = refs[:count], refs[count:]
        slot, m = pl.program_id(0), pl.program_id(1)
        me = (lax.axis_index("z") * 2 + lax.axis_index("core")) * owners + lax.axis_index("owner")
        live = table_ref[slot, me] >= 0

        @pl.when((slot == 0) & (m == 0))
        def _():
            for q in range(GROUPS * owners):
                for c in range(slots):
                    block = table_ref[c, q]
                    places[jnp.where(block >= 0, block, NBLOCKS)] = q * slots + c

        @pl.when(m == 0)
        def _():
            first = 0
            for part in parts:
                width = part.shape[-1]
                grad[:, first : first + width] = part[:, 0].reshape(size, width)
                first += width

        at = pl.ds(pl.multiple_of(m * tile, tile), tile)
        left = lax.dot_general(grad[at, :], grad[...], (((1,), (1,)), ((), ())), preferred_element_type=F32)
        right = lax.dot_general(grad[:, at], grad[...], (((0,), (0,)), ((), ())), preferred_element_type=F32)
        left_out[0] = jnp.where(live, left / size, 0.0).astype(BF16)
        right_out[0] = jnp.where(live, right / size, 0.0).astype(BF16)

    out = pl.BlockSpec((1, tile, size), lambda c, m: (c, m, 0))
    return pl.pallas_call(
        body,
        grid=(slots, size // tile),
        in_specs=[SMEM]
        + [pl.BlockSpec((owners, 1, rows, part.shape[-1]), lambda c, m: (0, c, 0, 0)) for part in arrived],
        out_specs=[out, out, SMEM],
        out_shape=[shape(slots, size, size)] * 2 + [jax.ShapeDtypeStruct((NBLOCKS + 1,), jnp.int32)],
        scratch_shapes=[pltpu.VMEM((size, size), BF16)],
        compiler_params=params(24),
        cost_estimate=cost(4 * slots * size**3, 6 * slots * size * size),
        name="gram_products",
    )(owner_blocks, *arrived)


def collect_update(places, received):
    owners, slots, rows, col = received.shape

    def body(place_ref, got_ref, out_ref):
        for block in range(NBLOCKS):
            out_ref[block] = got_ref[place_ref[block]]

    return pl.pallas_call(
        body,
        in_specs=[SMEM, VMEM],
        out_specs=VMEM,
        out_shape=shape(NBLOCKS, rows, col),
        compiler_params=params(16),
        cost_estimate=cost(0, 4 * NBLOCKS * rows * col * 2),
        name="collect_update",
    )(places, received.reshape(owners * slots, rows, col))


def local(partials, owner_blocks, left_root, right_root):
    partials = partials[0]
    left_root, right_root = left_root[0], right_root[0]
    _, rows, size = partials.shape
    owners = size // rows
    table = owner_blocks.T

    swap = [(0, 1), (1, 0)]
    up = [(z, (z + 1) % 4) for z in range(4)]
    down = [(z, (z - 1) % 4) for z in range(4)]

    def along_z(pair):
        return lax.ppermute(pair[0], "z", up), lax.ppermute(pair[1], "z", down)

    blocks, outgoing, outgoing_rest = gather_partner(table, partials)
    received = lax.ppermute(outgoing, "core", swap)
    own = gather_own(blocks, partials)
    outgoing_rest, received, own = lax.optimization_barrier((outgoing_rest, received, own))
    received_rest = lax.ppermute(outgoing_rest, "core", swap)

    def after(array, *earlier):
        return lax.optimization_barrier((array, *earlier))[0]

    *pair_a, wait_a, stay_a = add_pair(own[0], received, 0)
    got_a = along_z(pair_a)
    *pair_b, wait_b, stay_b = add_pair(after(own[1], stay_a), received_rest, 0)
    got_b = along_z(pair_b)
    late_a = add_waiting(after(wait_a, stay_b), *got_a)
    *pair_c, wait_c, stay_c = add_pair(after(own[2], late_a[0]), received_rest, SPLITS[1])
    late_a = along_z(late_a)
    got_c = along_z(lax.optimization_barrier((*pair_c, *got_b, *late_a)))
    picked_a = add_last_and_pick(table, [(after(stay_a, stay_c), *got_a, *late_a)])
    arrived = [lax.all_to_all(picked_a, "owner", split_axis=0, concat_axis=0, tiled=True)]
    late_b = add_waiting(after(wait_b, picked_a), *got_b)
    late_c = add_waiting(after(wait_c, late_b[0]), *got_c)
    late_b, late_c = along_z(late_b), along_z(late_c)
    picked = add_last_and_pick(table, [(stay_b, *got_b, *late_b), (stay_c, *got_c, *late_c)])
    arrived.append(lax.all_to_all(picked, "owner", split_axis=0, concat_axis=0, tiled=True))

    left_part = left_product(left_root, arrived[0])
    pieces = finish_update(left_root, right_root, left_part, arrived[1])
    pieces, arrived = lax.optimization_barrier((pieces, arrived))
    pieces = pieces.reshape(GROUPS * owners, 2, rows, 128)
    received = lax.all_to_all(pieces, ("z", "core", "owner"), split_axis=0, concat_axis=0, tiled=True)
    left_stat, right_stat, places = gram_products(table, arrived)
    update = collect_update(places, received)
    return left_stat[None], right_stat[None], update


def solution(mesh):
    mesh = Mesh(mesh.devices.reshape(4, 2, 16), ("z", "core", "owner"))
    dp = ("z", "core")
    owners = P(("z", "core", "owner"), None, None, None)
    in_specs = (P(dp, None, "owner", None), P(), owners, owners)
    out_specs = (owners, owners, P(None, "owner", dp))
    return jax.shard_map(local, mesh=mesh, in_specs=in_specs, out_specs=out_specs, check_vma=False)
```

time: 245 us -> 183 us (0.75)
  blocking collectives: 56.1 us -> 0 us
  Pallas kernels: 0 us -> 44.4 us
  starting transfers between devices: 8.18 us -> 45.6 us
  matrix products: 25.8 us -> 0 us
  local copies, waits for them, and re-layouts: 29 us -> 5.41 us
  other arithmetic: 20.5 us -> 0 us
  between operations: 14.3 us -> 0.81 us
  waiting for transfers between devices: 91 us -> 85.8 us
    all_to_all x1 -> x0, blocking collectives: 56.1 us -> none  [local(): lax.all_to_all(outgoing, 'owner', split_axis=1, concat_axis=1, tiled=True)]
    reduce_scatter x1 -> x0, waiting for transfers between devices: 54.3 us -> none  [local(): lax.psum_scatter(sorted_parts, 'dp', scatter_dimension=0, tiled=True)]
    pallas_call x0 -> x14, Pallas kernels: none -> 44.4 us  [the longest x1 14.3 us: gram_products(): pl.pallas_call(body, grid=(slots, size // tile), in_specs=[SMEM] + [pl.Bl...]
    all_to_all x1 -> x3, waiting for transfers between devices: 36.7 us -> 67.9 us  [the longest x1 37.3 us: local(): lax.all_to_all(pieces, ('z', 'core', 'owner'), split_axis=0, concat_axis=...]
    dot_general x6 -> x0, matrix products: 25.8 us -> none  [the longest x2 16.2 us: slot_products(): updated = jnp.dot(left_half, right_inv, preferred_element_type=jnp.float32)]
    all_to_all x1 -> x3, starting transfers between devices: 8.14 us -> 27.9 us  [the longest x1 14.5 us: local(): lax.all_to_all(pieces, ('z', 'core', 'owner'), split_axis=0, concat_axis=...]
    ppermute x0 -> x14, waiting for transfers between devices: none -> 17.9 us  [the longest x12 16.5 us: along_z(): return (lax.ppermute(pair[0], 'z', up), lax.ppermute(pair[1], 'z', down))]
    ppermute x0 -> x14, starting transfers between devices: none -> 17.7 us  [the longest x12 16.1 us: along_z(): return (lax.ppermute(pair[0], 'z', up), lax.ppermute(pair[1], 'z', down))]
  transfers between devices with their start and end apart: 2 -> 17, of which waited for: 2 -> 8; matrix products, arithmetic and copies ran while one was open for 6% -> 0% of each run, Pallas kernels for 0% -> 13%
where the time goes in v1:
time: 183 us; the launch traced here: 182 us
  waiting for transfers between devices  85.8 us (47%)
  starting transfers between devices  45.6 us (25%)
  Pallas kernels  44.4 us (24%)
  local copies, waits for them, and re-layouts  5.41 us (3%)
    all_to_all x1, waiting for transfers between devices, local(): lax.all_to_all(pieces, ('z', 'core', 'owner'), split_axis=0, concat_axis=...  37.3 us
    all_to_all x1, waiting for transfers between devices, local(): lax.all_to_all(picked, 'owner', split_axis=0, concat_axis=0, tiled=True)  30.6 us
    ppermute x12, waiting for transfers between devices, along_z(): return (lax.ppermute(pair[0], 'z', up), lax.ppermute(pair[1], 'z', down))  16.5 us
    ppermute x12, starting transfers between devices, along_z(): return (lax.ppermute(pair[0], 'z', up), lax.ppermute(pair[1], 'z', down))  16.1 us
    all_to_all x1, starting transfers between devices, local(): lax.all_to_all(pieces, ('z', 'core', 'owner'), split_axis=0, concat_axis=...  14.5 us
    pallas_call x1, Pallas kernels, gram_products(): pl.pallas_call(body, grid=(slots, size // tile), in_specs=[SMEM] + [pl.Bl...  14.3 us
    pallas_call x1, Pallas kernels, finish_update(): pl.pallas_call(body, in_specs=[HBM] * 4, out_specs=HBM, out_shape=shape(s...  12.7 us
    all_to_all x1, starting transfers between devices, local(): lax.all_to_all(picked_a, 'owner', split_axis=0, concat_axis=0, tiled=True)  6.77 us
  transfers between devices with their start and end apart: 17, of which 8 were waited for; matrix products, arithmetic and copies ran while one was open for 0% of the time, Pallas kernels for 13%

profile of v1, /device:TPU:1, one launch (start us, length us, event | category | flops | bytes accessed | tf_op | source)
XLA Modules:
  0.0 182.0 jit_solution(11683104413250032345)
XLA Ops:
  0.6 0.0 copy-start.2
  0.6 0.7 copy-done.2
  1.3 4.0 %gather_partner.1 = (s32[72]{0:T(128)S(1)}, bf16[32,64,256]{2,1,0:T(8,128)(2,1)S(1)}, bf16[32,64,768]{2,1,0:T(8,128)(2,1)S(1)}) custom-call(s32[2,128]{1,0:T(2,128)S(1)} %bitcast.10, bf16[64,64,1024]{2,1,0:T(8,128)(2,1)} %bitcast.14), custom_call_target="tpu_custom_call" | custom-call | bytes 8388608 | tf_op jit(solution)/shard_map/gather_partner/pallas_call | solution.py:77
  5.3 1.5 collective-permute-start
  6.8 2.8 %gather_own.1 = (bf16[32,64,256]{2,1,0:T(8,128)(2,1)S(1)}, bf16[32,64,256]{2,1,0:T(8,128)(2,1)S(1)}, bf16[32,64,512]{2,1,0:T(8,128)(2,1)S(1)}) custom-call(s32[72]{0:T(128)S(1)} %get-tuple-element.48.block_ref, bf16[64,64,1024]{2,1,0:T(8,128)(2,1)} %bitcast.15), custom_call_target="tpu_custom_call" | custom-call | bytes 8388608 | tf_op jit(solution)/shard_map/gather_own/pallas_call | solution.py:96
  9.6 0.0 collective-permute-done.got_ref
  9.6 0.1 collective-permute-start.1
  9.7 0.2 add_core_pair.3
  10.0 1.8 collective-permute-start.2
  11.8 2.2 %collective-permute-start.3 = (bf16[8,64,256]{2,1,0:T(8,128)(2,1)S(1)}, bf16[8,64,256]{2,1,0:T(8,128)(2,1)S(1)}, u32[]{:S(2)}, u32[]{:S(2)}) collective-permute-start(bf16[8,64,256]{2,1,0:T(8,128)(2,1)S(1)} %get-tuple-element.63), channel_id=1, source_target_pairs={{0,96},{32,0},{64,32},{96,64},{1,97},{33,1},{65,33},{97,65},{2,98}... | collective-permute-start | bytes 786440 | tf_op jit(solution)/shard_map/ppermute | solution.py:344
  14.0 0.0 copy-start.3
  14.0 1.4 collective-permute-done.1.got_ref
  15.4 0.9 add_core_pair.4
  16.2 3.9 %collective-permute-done.2.up_ref.refs_1_ = bf16[8,64,256]{2,1,0:T(8,128)(2,1)S(1)} collective-permute-done((bf16[8,64,256]{2,1,0:T(8,128)(2,1)S(1)}, bf16[8,64,256]{2,1,0:T(8,128)(2,1)S(1)}, u32[]{:S(2)}, u32[]{:S(2)}) %collective-permute-start.2) | collective-permute-done | bytes 262176 | tf_op jit(solution)/shard_map/ppermute | solution.py:344
  20.1 0.0 collective-permute-done.3.down_ref.refs_2_
  20.1 0.1 add_waiting.3
  20.2 2.5 %collective-permute-start.5 = (bf16[4,64,256]{2,1,0:T(8,128)(2,1)S(1)}, bf16[4,64,256]{2,1,0:T(8,128)(2,1)S(1)}, u32[]{:S(2)}, u32[]{:S(2)}) collective-permute-start(bf16[4,64,256]{2,1,0:T(8,128)(2,1)S(1)} %get-tuple-element.68), channel_id=1, source_target_pairs={{0,96},{32,0},{64,32},{96,64},{1,97},{33,1},{65,33},{97,65},{2,98}... | collective-permute-start | bytes 393224 | tf_op jit(solution)/shard_map/ppermute | solution.py:344
  22.7 0.0 collective-permute-start.4
  22.7 0.0 collective-permute-start.6
  22.7 2.7 %collective-permute-start.7 = (bf16[8,64,256]{2,1,0:T(8,128)(2,1)S(1)}, bf16[8,64,256]{2,1,0:T(8,128)(2,1)S(1)}, u32[]{:S(2)}, u32[]{:S(2)}) collective-permute-start(bf16[8,64,256]{2,1,0:T(8,128)(2,1)S(1)} %get-tuple-element.70), channel_id=1, source_target_pairs={{0,96},{32,0},{64,32},{96,64},{1,97},{33,1},{65,33},{97,65},{2,98}... | collective-permute-start | bytes 786440 | tf_op jit(solution)/shard_map/ppermute | solution.py:344
  25.4 0.5 add_core_pair.5
  25.9 0.0 copy-start.4
  25.9 0.8 copy-done.4
  26.7 0.0 copy-start.5
  26.7 0.8 copy-done.5
  27.5 0.0 collective-permute-done.5.refs_4_
  27.5 0.2 collective-permute-done.4.refs_3_
  27.7 0.0 copy-done.3
  27.7 1.6 add_last_and_pick.2
  29.3 6.8 %all-to-all-start = ((bf16[16,2,64,256]{3,2,1,0:T(8,128)(2,1)}), bf16[16,2,64,256]{3,2,1,0:T(8,128)(2,1)S(1)}, u32[]{:S(2)}, u32[]{:S(2)}) async-start(bf16[16,2,64,256]{3,2,1,0:T(8,128)(2,1)} %add_last_and_pick.2), calls=%async_computation | async-start | bytes 2097152 | tf_op jit(solution)/shard_map/all_to_all | solution.py:364
  36.1 0.0 collective-permute-done.6.up_ref.refs_1_
  36.1 0.0 collective-permute-done.7.down_ref.refs_2_
  36.1 0.1 collective-permute-start.10
  36.2 2.7 %collective-permute-start.11 = (bf16[8,64,512]{2,1,0:T(8,128)(2,1)}, bf16[8,64,512]{2,1,0:T(8,128)(2,1)S(1)}, u32[]{:S(2)}, u32[]{:S(2)}) collective-permute-start(bf16[8,64,512]{2,1,0:T(8,128)(2,1)} %copy-done.4), channel_id=1, source_target_pairs={{0,96},{32,0},{64,32},{96,64},{1,97},{33,1},{65,33},{97,65},{2,98}... | collective-permute-start | bytes 1572872 | tf_op jit(solution)/shard_map/ppermute | solution.py:344
  38.9 0.1 add_waiting.4
  38.9 7.6 %collective-permute-done.10.up_ref.refs_6_ = bf16[8,64,512]{2,1,0:T(8,128)(2,1)S(1)} collective-permute-done((bf16[8,64,512]{2,1,0:T(8,128)(2,1)}, bf16[8,64,512]{2,1,0:T(8,128)(2,1)S(1)}, u32[]{:S(2)}, u32[]{:S(2)}) %collective-permute-start.10) | collective-permute-done | bytes 524320 | tf_op jit(solution)/shard_map/ppermute | solution.py:344
  46.5 0.0 collective-permute-done.11.down_ref.refs_7_
  46.5 0.1 add_waiting.5
  46.6 1.2 collective-permute-start.12
  47.9 1.5 collective-permute-start.13
  49.4 1.2 collective-permute-start.9
  50.6 0.3 collective-permute-start.8
  50.9 4.2 %collective-permute-done.9.refs_4_ = bf16[4,64,256]{2,1,0:T(8,128)(2,1)S(1)} collective-permute-done((bf16[4,64,256]{2,1,0:T(8,128)(2,1)S(1)}, bf16[4,64,256]{2,1,0:T(8,128)(2,1)S(1)}, u32[]{:S(2)}, u32[]{:S(2)}) %collective-permute-start.9) | collective-permute-done | bytes 131104 | tf_op jit(solution)/shard_map/ppermute | solution.py:344
  55.0 0.6 collective-permute-done.8.refs_3_
  55.6 0.0 collective-permute-done.12.refs_8_
  55.6 0.0 collective-permute-done.13.refs_9_
  55.6 2.5 %add_last_and_pick.3 = bf16[16,2,64,768]{3,2,1,0:T(8,128)(2,1)} custom-call(s32[2,128]{1,0:T(2,128)S(1)} %bitcast.12, bf16[8,64,256]{2,1,0:T(8,128)(2,1)S(1)} %get-tuple-element.60.refs_0_, bf16[8,64,256]{2,1,0:T(8,128)(2,1)S(1)} %collective-permute-done.6.up_ref.refs_1_, bf16[8,64,256]{2,1,0:T(8,128)(2,1)S(1)} %collective-permute-done.7.down_ref.refs_2_, ...), custom_call_target="tpu_custom_call" | custom-call | bytes 5505024 | tf_op jit(solution)/shard_map/add_last_and_pick/pallas_call | solution.py:170
  58.1 0.0 all-to-all-done.grad_ref.refs_0_
  58.1 6.6 %all-to-all-start.1 = ((bf16[16,2,64,768]{3,2,1,0:T(8,128)(2,1)}), bf16[16,2,64,768]{3,2,1,0:T(8,128)(2,1)}, u32[]{:S(2)}, u32[]{:S(2)}) async-start(bf16[16,2,64,768]{3,2,1,0:T(8,128)(2,1)} %add_last_and_pick.3), calls=%async_computation.1 | async-start | bytes 6291456 | tf_op jit(solution)/shard_map/all_to_all | solution.py:369
  64.7 0.0 copy-start
  64.7 2.2 %copy-done = bf16[1,2,1024,1024]{3,2,1,0:T(8,128)(2,1)S(1)} copy-done((bf16[1,2,1024,1024]{3,2,1,0:T(8,128)(2,1)S(1)}, bf16[1,2,1024,1024]{3,2,1,0:T(8,128)(2,1)}, u32[]{:S(2)}) %copy-start) | copy-done | bytes 4194328
  66.9 1.5 left_product.1.part_ref
  68.4 0.0 copy-start.1
  68.4 1.0 copy-done.1
  69.4 30.6 %all-to-all-done.1.grad_ref.refs_1_ = bf16[16,2,64,768]{3,2,1,0:T(8,128)(2,1)} async-done(((bf16[16,2,64,768]{3,2,1,0:T(8,128)(2,1)}), bf16[16,2,64,768]{3,2,1,0:T(8,128)(2,1)}, u32[]{:S(2)}, u32[]{:S(2)}) %all-to-all-start.1) | async-done | bytes 3145760 | tf_op jit(solution)/shard_map/all_to_all | solution.py:369
  100.0 12.7 %finish_update.1 = bf16[8,16,2,64,128]{4,3,2,1,0:T(8,128)(2,1)} custom-call(bf16[2,1024,1024]{2,1,0:T(8,128)(2,1)} %bitcast.8, bf16[2,1024,1024]{2,1,0:T(8,128)(2,1)} %bitcast.17, bf16[2,1024,256]{2,1,0:T(8,128)(2,1)} %copy-done.1, bf16[16,2,64,768]{3,2,1,0:T(8,128)(2,1)} %all-to-all-done.1.grad_ref.refs_1_), custom_call_target="tpu_custom_call" | custom-call | flops 7516192768 | bytes 12582912 | tf_op jit(solution)/shard_map/finish_update/pallas_call | solution.py:245
  112.7 14.5 %all-to-all-start.2 = ((bf16[128,2,64,128]{3,2,1,0:T(8,128)(2,1)}), bf16[128,2,64,128]{3,2,1,0:T(8,128)(2,1)}, u32[]{:S(2)}, u32[]{:S(2)}) async-start(bf16[128,2,64,128]{3,2,1,0:T(8,128)(2,1)} %bitcast.16), calls=%async_computation.2 | async-start | bytes 8388608 | tf_op jit(solution)/shard_map/all_to_all | solution.py:375
  127.2 14.3 %gram_products.1 = (bf16[2,1024,1024]{2,1,0:T(8,128)(2,1)}, bf16[2,1024,1024]{2,1,0:T(8,128)(2,1)}, s32[65]{0:T(128)S(1)}) custom-call(s32[2,128]{1,0:T(2,128)S(1)} %bitcast.13, bf16[16,2,64,256]{3,2,1,0:T(8,128)(2,1)S(1)} %all-to-all-done.grad_ref.refs_0_, bf16[16,2,64,768]{3,2,1,0:T(8,128)(2,1)} %all-to-all-done.1.grad_ref.refs_1_), custom_call_target="tpu_custom_call" | custom-call | flops 8589934592 | bytes 12582912 | tf_op jit(solution)/shard_map/gram_products/pallas_call | solution.py:300
  141.5 37.3 %all-to-all-done.2 = bf16[128,2,64,128]{3,2,1,0:T(8,128)(2,1)} async-done(((bf16[128,2,64,128]{3,2,1,0:T(8,128)(2,1)}), bf16[128,2,64,128]{3,2,1,0:T(8,128)(2,1)}, u32[]{:S(2)}, u32[]{:S(2)}) %all-to-all-start.2) | async-done | bytes 4194336 | tf_op jit(solution)/shard_map/all_to_all | solution.py:375
  178.8 3.2 %collect_update.1 = bf16[64,64,128]{2,1,0:T(8,128)(2,1)} custom-call(s32[65]{0:T(128)S(1)} %get-tuple-element.87.place_ref, bf16[256,64,128]{2,1,0:T(8,128)(2,1)} %bitcast.7.got_ref), custom_call_target="tpu_custom_call" | custom-call | bytes 4194304 | tf_op jit(solution)/shard_map/collect_update/pallas_call | solution.py:321
Async XLA Ops:
  0.6 0.7 copy-start.2
  5.3 4.3 %collective-permute-start = (bf16[32,64,256]{2,1,0:T(8,128)(2,1)S(1)}, bf16[32,64,256]{2,1,0:T(8,128)(2,1)S(1)}, u32[]{:S(2)}, u32[]{:S(2)}) collective-permute-start(bf16[32,64,256]{2,1,0:T(8,128)(2,1)S(1)} %get-tuple-element.47), channel_id=1, source_target_pairs={{0,16},{16,0},{1,17},{17,1},{2,18},{18,2},{3,19},{19,3},{4,20},{20... | collective-permute-start | bytes 3145736 | tf_op jit(solution)/shard_map/ppermute | solution.py:347
  9.6 5.7 %collective-permute-start.1 = (bf16[32,64,768]{2,1,0:T(8,128)(2,1)S(1)}, bf16[32,64,768]{2,1,0:T(8,128)(2,1)S(1)}, u32[]{:S(2)}, u32[]{:S(2)}) collective-permute-start(bf16[32,64,768]{2,1,0:T(8,128)(2,1)S(1)} %get-tuple-element.59), channel_id=1, source_target_pairs={{0,16},{16,0},{1,17},{17,1},{2,18},{18,2},{3,19},{19,3},{4,20},{20... | collective-permute-start | bytes 9437192 | tf_op jit(solution)/shard_map/ppermute | solution.py:350
  10.0 10.2 %collective-permute-start.2 = (bf16[8,64,256]{2,1,0:T(8,128)(2,1)S(1)}, bf16[8,64,256]{2,1,0:T(8,128)(2,1)S(1)}, u32[]{:S(2)}, u32[]{:S(2)}) collective-permute-start(bf16[8,64,256]{2,1,0:T(8,128)(2,1)S(1)} %get-tuple-element.62), channel_id=1, source_target_pairs={{0,32},{32,64},{64,96},{96,0},{1,33},{33,65},{65,97},{97,1},{2,34}... | collective-permute-start | bytes 786440 | tf_op jit(solution)/shard_map/ppermute | solution.py:344
  11.8 8.4 %collective-permute-start.3 = (bf16[8,64,256]{2,1,0:T(8,128)(2,1)S(1)}, bf16[8,64,256]{2,1,0:T(8,128)(2,1)S(1)}, u32[]{:S(2)}, u32[]{:S(2)}) collective-permute-start(bf16[8,64,256]{2,1,0:T(8,128)(2,1)S(1)} %get-tuple-element.63), channel_id=1, source_target_pairs={{0,96},{32,0},{64,32},{96,64},{1,97},{33,1},{65,33},{97,65},{2,98}... | collective-permute-start | bytes 786440 | tf_op jit(solution)/shard_map/ppermute | solution.py:344
  14.0 13.8 %copy-start.3 = (s32[128,2]{0,1:T(2,128)S(1)}, s32[128,2]{0,1:T(2,128)}, u32[]{:S(2)}) copy-start(s32[128,2]{0,1:T(2,128)} %param.5) | copy-start | bytes 3076
  20.2 7.3 %collective-permute-start.5 = (bf16[4,64,256]{2,1,0:T(8,128)(2,1)S(1)}, bf16[4,64,256]{2,1,0:T(8,128)(2,1)S(1)}, u32[]{:S(2)}, u32[]{:S(2)}) collective-permute-start(bf16[4,64,256]{2,1,0:T(8,128)(2,1)S(1)} %get-tuple-element.68), channel_id=1, source_target_pairs={{0,96},{32,0},{64,32},{96,64},{1,97},{33,1},{65,33},{97,65},{2,98}... | collective-permute-start | bytes 393224 | tf_op jit(solution)/shard_map/ppermute | solution.py:344
  22.7 5.0 %collective-permute-start.4 = (bf16[4,64,256]{2,1,0:T(8,128)(2,1)S(1)}, bf16[4,64,256]{2,1,0:T(8,128)(2,1)S(1)}, u32[]{:S(2)}, u32[]{:S(2)}) collective-permute-start(bf16[4,64,256]{2,1,0:T(8,128)(2,1)S(1)} %get-tuple-element.64), channel_id=1, source_target_pairs={{0,32},{32,64},{64,96},{96,0},{1,33},{33,65},{65,97},{97,1},{2,34}... | collective-permute-start | bytes 393224 | tf_op jit(solution)/shard_map/ppermute | solution.py:344
  22.7 13.4 %collective-permute-start.6 = (bf16[8,64,256]{2,1,0:T(8,128)(2,1)}, bf16[8,64,256]{2,1,0:T(8,128)(2,1)S(1)}, u32[]{:S(2)}, u32[]{:S(2)}) collective-permute-start(bf16[8,64,256]{2,1,0:T(8,128)(2,1)} %get-tuple-element.69), channel_id=1, source_target_pairs={{0,32},{32,64},{64,96},{96,0},{1,33},{33,65},{65,97},{97,1},{2,34}... | collective-permute-start | bytes 786440 | tf_op jit(solution)/shard_map/ppermute | solution.py:344
  22.7 13.4 %collective-permute-start.7 = (bf16[8,64,256]{2,1,0:T(8,128)(2,1)S(1)}, bf16[8,64,256]{2,1,0:T(8,128)(2,1)S(1)}, u32[]{:S(2)}, u32[]{:S(2)}) collective-permute-start(bf16[8,64,256]{2,1,0:T(8,128)(2,1)S(1)} %get-tuple-element.70), channel_id=1, source_target_pairs={{0,96},{32,0},{64,32},{96,64},{1,97},{33,1},{65,33},{97,65},{2,98}... | collective-permute-start | bytes 786440 | tf_op jit(solution)/shard_map/ppermute | solution.py:344
  25.9 0.8 copy-start.4
  26.7 0.8 copy-start.5
  29.3 28.8 %all-to-all-start = ((bf16[16,2,64,256]{3,2,1,0:T(8,128)(2,1)}), bf16[16,2,64,256]{3,2,1,0:T(8,128)(2,1)S(1)}, u32[]{:S(2)}, u32[]{:S(2)}) async-start(bf16[16,2,64,256]{3,2,1,0:T(8,128)(2,1)} %add_last_and_pick.2), calls=%async_computation | async-start | bytes 2097152 | tf_op jit(solution)/shard_map/all_to_all | solution.py:364
  36.1 10.4 %collective-permute-start.10 = (bf16[8,64,512]{2,1,0:T(8,128)(2,1)}, bf16[8,64,512]{2,1,0:T(8,128)(2,1)S(1)}, u32[]{:S(2)}, u32[]{:S(2)}) collective-permute-start(bf16[8,64,512]{2,1,0:T(8,128)(2,1)} %copy-done.5), channel_id=1, source_target_pairs={{0,32},{32,64},{64,96},{96,0},{1,33},{33,65},{65,97},{97,1},{2,34}... | collective-permute-start | bytes 1572872 | tf_op jit(solution)/shard_map/ppermute | solution.py:344
  36.2 10.3 %collective-permute-start.11 = (bf16[8,64,512]{2,1,0:T(8,128)(2,1)}, bf16[8,64,512]{2,1,0:T(8,128)(2,1)S(1)}, u32[]{:S(2)}, u32[]{:S(2)}) collective-permute-start(bf16[8,64,512]{2,1,0:T(8,128)(2,1)} %copy-done.4), channel_id=1, source_target_pairs={{0,96},{32,0},{64,32},{96,64},{1,97},{33,1},{65,33},{97,65},{2,98}... | collective-permute-start | bytes 1572872 | tf_op jit(solution)/shard_map/ppermute | solution.py:344
  46.6 9.0 %collective-permute-start.12 = (bf16[4,64,512]{2,1,0:T(8,128)(2,1)S(1)}, bf16[4,64,512]{2,1,0:T(8,128)(2,1)S(1)}, u32[]{:S(2)}, u32[]{:S(2)}) collective-permute-start(bf16[4,64,512]{2,1,0:T(8,128)(2,1)S(1)} %get-tuple-element.81), channel_id=1, source_target_pairs={{0,32},{32,64},{64,96},{96,0},{1,33},{33,65},{65,97},{97,1},{2,34}... | collective-permute-start | bytes 786440 | tf_op jit(solution)/shard_map/ppermute | solution.py:344
  47.9 7.7 %collective-permute-start.13 = (bf16[4,64,512]{2,1,0:T(8,128)(2,1)S(1)}, bf16[4,64,512]{2,1,0:T(8,128)(2,1)S(1)}, u32[]{:S(2)}, u32[]{:S(2)}) collective-permute-start(bf16[4,64,512]{2,1,0:T(8,128)(2,1)S(1)} %get-tuple-element.82), channel_id=1, source_target_pairs={{0,96},{32,0},{64,32},{96,64},{1,97},{33,1},{65,33},{97,65},{2,98}... | collective-permute-start | bytes 786440 | tf_op jit(solution)/shard_map/ppermute | solution.py:344
  49.4 5.6 %collective-permute-start.9 = (bf16[4,64,256]{2,1,0:T(8,128)(2,1)S(1)}, bf16[4,64,256]{2,1,0:T(8,128)(2,1)S(1)}, u32[]{:S(2)}, u32[]{:S(2)}) collective-permute-start(bf16[4,64,256]{2,1,0:T(8,128)(2,1)S(1)} %get-tuple-element.74), channel_id=1, source_target_pairs={{0,96},{32,0},{64,32},{96,64},{1,97},{33,1},{65,33},{97,65},{2,98}... | collective-permute-start | bytes 393224 | tf_op jit(solution)/shard_map/ppermute | solution.py:344
  50.6 5.0 %collective-permute-start.8 = (bf16[4,64,256]{2,1,0:T(8,128)(2,1)S(1)}, bf16[4,64,256]{2,1,0:T(8,128)(2,1)S(1)}, u32[]{:S(2)}, u32[]{:S(2)}) collective-permute-start(bf16[4,64,256]{2,1,0:T(8,128)(2,1)S(1)} %get-tuple-element.73), channel_id=1, source_target_pairs={{0,32},{32,64},{64,96},{96,0},{1,33},{33,65},{65,97},{97,1},{2,34}... | collective-permute-start | bytes 393224 | tf_op jit(solution)/shard_map/ppermute | solution.py:344
  58.1 41.9 %all-to-all-start.1 = ((bf16[16,2,64,768]{3,2,1,0:T(8,128)(2,1)}), bf16[16,2,64,768]{3,2,1,0:T(8,128)(2,1)}, u32[]{:S(2)}, u32[]{:S(2)}) async-start(bf16[16,2,64,768]{3,2,1,0:T(8,128)(2,1)} %add_last_and_pick.3), calls=%async_computation.1 | async-start | bytes 6291456 | tf_op jit(solution)/shard_map/all_to_all | solution.py:369
  64.7 2.2 %copy-start = (bf16[1,2,1024,1024]{3,2,1,0:T(8,128)(2,1)S(1)}, bf16[1,2,1024,1024]{3,2,1,0:T(8,128)(2,1)}, u32[]{:S(2)}) copy-start(bf16[1,2,1024,1024]{3,2,1,0:T(8,128)(2,1)} %param.6) | copy-start | bytes 12582916
  68.4 1.0 copy-start.1
  112.7 66.1 %all-to-all-start.2 = ((bf16[128,2,64,128]{3,2,1,0:T(8,128)(2,1)}), bf16[128,2,64,128]{3,2,1,0:T(8,128)(2,1)}, u32[]{:S(2)}, u32[]{:S(2)}) async-start(bf16[128,2,64,128]{3,2,1,0:T(8,128)(2,1)} %bitcast.16), calls=%async_computation.2 | async-start | bytes 8388608 | tf_op jit(solution)/shard_map/all_to_all | solution.py:375

commit v2 on v1

--- a/solution.py
+++ b/solution.py
@@ -5,7 +5,8 @@
 from jax.experimental.pallas import tpu as pltpu
 from jax.sharding import Mesh, PartitionSpec as P
 
-SPLITS = (256, 256, 512)
+SPLITS = (256, 384, 384)
+TILE = 128
 GROUPS = 8
 NBLOCKS = 64
 F32 = jnp.float32
@@ -53,9 +54,8 @@
             rank[g] = rank[g] + (block >= 0).astype(jnp.int32)
 
 
-def copy_blocks(blocks, core, part_ref, outs, sems):
+def copy_blocks(blocks, core, part_ref, first, outs, sems):
     numbers = [blocks[place] for place in wanted(core)]
-    first = 0
     copies = []
     for k, out in enumerate(outs):
         columns = pl.ds(first, out.shape[-1])
@@ -63,45 +63,50 @@
             pltpu.make_async_copy(part_ref.at[block, :, columns], out.at[j], sems.at[k]).start()
         copies.append(pltpu.make_async_copy(part_ref.at[pl.ds(0, 32), :, columns], out, sems.at[k]))
         first += out.shape[-1]
-    for copy in copies:
-        copy.wait()
-
-
-def gather_partner(owner_blocks, partials):
+    return copies
+
+
+def gather_first(owner_blocks, partials):
+    rows = partials.shape[1]
+
+    def body(table_ref, part_ref, blocks, out, sems):
+        block_table(table_ref, blocks)
+        for copy in copy_blocks(blocks, 1 - lax.axis_index("core"), part_ref, 0, [out], sems):
+            copy.wait()
+
+    return pl.pallas_call(
+        body,
+        in_specs=[SMEM, HBM],
+        out_specs=[SMEM, VMEM],
+        out_shape=[jax.ShapeDtypeStruct((GROUPS * 9,), jnp.int32), shape(32, rows, SPLITS[0])],
+        scratch_shapes=[pltpu.SemaphoreType.DMA((1,))],
+        compiler_params=params(50),
+        cost_estimate=cost(0, 2 * 32 * rows * SPLITS[0] * 2),
+        name="gather_first",
+    )(owner_blocks, partials)
+
+
+def gather_rest(blocks, partials):
     rows, size = partials.shape[1:]
-
-    def body(table_ref, part_ref, blocks, *refs):
-        block_table(table_ref, blocks)
-        copy_blocks(blocks, 1 - lax.axis_index("core"), part_ref, refs[:-1], refs[-1])
+    widths = (*SPLITS, size - SPLITS[0])
+
+    def body(block_ref, part_ref, *refs):
+        *own, other, sems = refs
+        core = lax.axis_index("core")
+        copies = copy_blocks(block_ref, core, part_ref, 0, own, sems)
+        copies += copy_blocks(block_ref, 1 - core, part_ref, SPLITS[0], [other], sems.at[pl.ds(len(own), 1)])
+        for copy in copies:
+            copy.wait()
 
     return pl.pallas_call(
         body,
         in_specs=[SMEM, HBM],
-        out_specs=[SMEM, VMEM, VMEM],
-        out_shape=[jax.ShapeDtypeStruct((GROUPS * 9,), jnp.int32)]
-        + [shape(32, rows, w) for w in (SPLITS[0], size - SPLITS[0])],
-        scratch_shapes=[pltpu.SemaphoreType.DMA((2,))],
-        compiler_params=params(48),
-        cost_estimate=cost(0, 2 * 32 * rows * size * 2),
-        name="gather_partner",
-    )(owner_blocks, partials)
-
-
-def gather_own(blocks, partials):
-    rows, size = partials.shape[1:]
-
-    def body(block_ref, part_ref, *refs):
-        copy_blocks(block_ref, lax.axis_index("core"), part_ref, refs[:-1], refs[-1])
-
-    return pl.pallas_call(
-        body,
-        in_specs=[SMEM, HBM],
-        out_specs=[VMEM] * len(SPLITS),
-        out_shape=[shape(32, rows, w) for w in SPLITS],
-        scratch_shapes=[pltpu.SemaphoreType.DMA((len(SPLITS),))],
+        out_specs=[VMEM] * len(widths),
+        out_shape=[shape(32, rows, w) for w in widths],
+        scratch_shapes=[pltpu.SemaphoreType.DMA((len(widths),))],
         compiler_params=params(44),
-        cost_estimate=cost(0, 2 * 32 * rows * size * 2),
-        name="gather_own",
+        cost_estimate=cost(0, 2 * 32 * rows * sum(widths) * 2),
+        name="gather_rest",
     )(blocks, partials)
 
 
@@ -125,58 +130,120 @@
     )(own, received)
 
 
-def add_waiting(waiting, got_up, got_down):
-    _, rows, width = waiting.shape
-
-    def body(wait_ref, up_ref, down_ref, up_out, down_out):
+def cols(tile):
+    return slice(tile * TILE, (tile + 1) * TILE)
+
+
+def mix_first_second(waiting, got_up, got_down, own, received):
+    _, rows, width = own.shape
+    late, tiles = waiting.shape[2] // TILE, width // TILE
+    head = 4 * late
+
+    def body(wait_ref, up_ref, down_ref, own_ref, got_ref, up_out, down_out, wait_out, stay_out):
         for t in range(4):
-            up_out[t] = add(wait_ref[t], up_ref[t])
-            down_out[t] = add(wait_ref[4 + t], down_ref[t])
-
-    return pl.pallas_call(
-        body,
-        in_specs=[VMEM] * 3,
+            for n in range(late):
+                up_out[late * t + n] = add(wait_ref[t, :, cols(n)], up_ref[t, :, cols(n)])
+                down_out[late * t + n] = add(wait_ref[4 + t, :, cols(n)], down_ref[t, :, cols(n)])
+        for t in range(8):
+            for n in range(tiles):
+                up_out[head + tiles * t + n] = add(own_ref[t, :, cols(n)], got_ref[t, :, cols(n)])
+                down_out[head + tiles * t + n] = add(own_ref[8 + t, :, cols(n)], got_ref[8 + t, :, cols(n)])
+            wait_out[t] = add(own_ref[16 + t], got_ref[16 + t, :, :width])
+            stay_out[t] = add(own_ref[24 + t], got_ref[24 + t, :, :width])
+
+    mixed = shape(head + 8 * tiles, rows, TILE)
+    return pl.pallas_call(
+        body,
+        in_specs=[VMEM] * 5,
+        out_specs=[VMEM] * 4,
+        out_shape=[mixed, mixed, shape(8, rows, width), shape(8, rows, width)],
+        compiler_params=params(16),
+        cost_estimate=cost(0, 3 * 32 * rows * width * 2),
+        name="mix_first_second",
+    )(waiting, got_up, got_down, own, received)
+
+
+def add_waiting(wait_b, mixed_up, mixed_down, wait_c, got_up, got_down):
+    _, rows, width_b = wait_b.shape
+    width_c = wait_c.shape[2]
+    tiles = width_b // TILE
+    head = mixed_up.shape[0] - 8 * tiles
+
+    def body(b_ref, mixed_up_ref, mixed_down_ref, c_ref, up_ref, down_ref, up_out, down_out):
+        for t in range(4):
+            for n in range(tiles):
+                up_out[t, :, cols(n)] = add(b_ref[t, :, cols(n)], mixed_up_ref[head + tiles * t + n])
+                down_out[t, :, cols(n)] = add(b_ref[4 + t, :, cols(n)], mixed_down_ref[head + tiles * t + n])
+            up_out[t, :, width_b:] = add(c_ref[t], up_ref[t])
+            down_out[t, :, width_b:] = add(c_ref[4 + t], down_ref[t])
+
+    return pl.pallas_call(
+        body,
+        in_specs=[VMEM] * 6,
         out_specs=[VMEM] * 2,
-        out_shape=[shape(4, rows, width)] * 2,
+        out_shape=[shape(4, rows, width_b + width_c)] * 2,
         compiler_params=params(16),
-        cost_estimate=cost(0, 24 * rows * width * 2),
+        cost_estimate=cost(10**12, 10**9),
         name="add_waiting",
-    )(waiting, got_up, got_down)
-
-
-def add_last_and_pick(owner_blocks, chunks):
-    rows = chunks[0][0].shape[1]
-    widths = [chunk[0].shape[2] for chunk in chunks]
-
-    def body(table_ref, *refs):
-        ins, (out_ref, total, sem) = refs[:-3], refs[-3:]
-        first = 0
-        for k, width in enumerate(widths):
-            own_ref, up_ref, down_ref, late_up_ref, late_down_ref = ins[5 * k : 5 * k + 5]
-            columns = slice(first, first + width)
-            for t in range(4):
-                total[t, :, columns] = add(own_ref[t], late_up_ref[t], down_ref[4 + t])
-                total[4 + t, :, columns] = add(own_ref[4 + t], late_down_ref[t], up_ref[4 + t])
-            first += width
-        start = (lax.axis_index("z") * 2 + lax.axis_index("core")) * 16
-        rank = jnp.int32(0)
-        for slot in range(32):
-            pltpu.make_async_copy(
-                total.at[jnp.minimum(rank, 7)], out_ref.at[slot // 2, slot % 2], sem
-            ).start()
-            rank = rank + (table_ref[slot % 2, start + slot // 2] >= 0).astype(jnp.int32)
-        pltpu.make_async_copy(out_ref, out_ref, sem).wait()
-
-    return pl.pallas_call(
-        body,
-        in_specs=[SMEM] + [VMEM] * (5 * len(chunks)),
+    )(wait_b, mixed_up, mixed_down, wait_c, got_up, got_down)
+
+
+def pick_slots(table_ref, total, out_ref, sem):
+    start = (lax.axis_index("z") * 2 + lax.axis_index("core")) * 16
+    rank = jnp.int32(0)
+    for slot in range(32):
+        pltpu.make_async_copy(total.at[jnp.minimum(rank, 7)], out_ref.at[slot // 2, slot % 2], sem).start()
+        rank = rank + (table_ref[slot % 2, start + slot // 2] >= 0).astype(jnp.int32)
+    pltpu.make_async_copy(out_ref, out_ref, sem).wait()
+
+
+def last_call(body, owner_blocks, arrays, rows, width):
+    return pl.pallas_call(
+        body,
+        in_specs=[SMEM] + [VMEM] * len(arrays),
         out_specs=HBM,
-        out_shape=shape(16, 2, rows, sum(widths)),
-        scratch_shapes=[pltpu.VMEM((8, rows, sum(widths)), BF16), pltpu.SemaphoreType.DMA],
+        out_shape=shape(16, 2, rows, width),
+        scratch_shapes=[pltpu.VMEM((8, rows, width), BF16), pltpu.SemaphoreType.DMA],
         compiler_params=params(16),
-        cost_estimate=cost(0, 56 * rows * sum(widths) * 2),
+        cost_estimate=cost(0, 56 * rows * width * 2),
         name="add_last_and_pick",
-    )(owner_blocks, *[array for chunk in chunks for array in chunk])
+    )(owner_blocks, *arrays)
+
+
+def last_of_first(owner_blocks, stay, got_up, got_down, mixed_up, mixed_down):
+    _, rows, width = stay.shape
+    late = width // TILE
+
+    def body(table_ref, own_ref, up_ref, down_ref, mixed_up_ref, mixed_down_ref, out_ref, total, sem):
+        for t in range(4):
+            for n in range(late):
+                at = cols(n)
+                total[t, :, at] = add(own_ref[t, :, at], mixed_up_ref[late * t + n], down_ref[4 + t, :, at])
+                total[4 + t, :, at] = add(own_ref[4 + t, :, at], mixed_down_ref[late * t + n], up_ref[4 + t, :, at])
+        pick_slots(table_ref, total, out_ref, sem)
+
+    return last_call(body, owner_blocks, (stay, got_up, got_down, mixed_up, mixed_down), rows, width)
+
+
+def last_of_rest(owner_blocks, stay_b, mixed_up, mixed_down, stay_c, got_up, got_down, late_up, late_down):
+    _, rows, width = late_up.shape
+    width_b = stay_b.shape[2]
+    tiles = width_b // TILE
+    head = mixed_up.shape[0] - 8 * tiles
+
+    def body(table_ref, b_ref, mixed_up_ref, mixed_down_ref, c_ref, up_ref, down_ref, late_up_ref, late_down_ref,
+             out_ref, total, sem):
+        for t in range(4):
+            for n in range(tiles):
+                at, high = cols(n), head + tiles * (4 + t) + n
+                total[t, :, at] = add(b_ref[t, :, at], late_up_ref[t, :, at], mixed_down_ref[high])
+                total[4 + t, :, at] = add(b_ref[4 + t, :, at], late_down_ref[t, :, at], mixed_up_ref[high])
+            total[t, :, width_b:] = add(c_ref[t], late_up_ref[t, :, width_b:], down_ref[4 + t])
+            total[4 + t, :, width_b:] = add(c_ref[4 + t], late_down_ref[t, :, width_b:], up_ref[4 + t])
+        pick_slots(table_ref, total, out_ref, sem)
+
+    arrays = (stay_b, mixed_up, mixed_down, stay_c, got_up, got_down, late_up, late_down)
+    return last_call(body, owner_blocks, arrays, rows, width)
 
 
 def left_product(left_root, arrived):
@@ -206,32 +273,36 @@
     owners, slots, rows, width = arrived.shape
     size = owners * rows
     done = size - width
-    tile, col = 256, 128
-    cuts = [(at, min(tile, width - at)) for at in range(0, width, tile)]
+    tile, col = 512, 128
     per = tile // col
 
     def body(left_ref, right_ref, part_ref, grad_ref, out_ref, left, right, part, grad, half, out, sems, out_sem):
         copies = {}
 
-        def fetch(name, source, target):
-            copies[name] = pltpu.make_async_copy(source, target, sems.at[len(copies)])
-            copies[name].start()
-
+        def fetch(c, *names):
+            pairs = {
+                "left": (left_ref.at[c], left.at[c]),
+                "grad": (grad_ref.at[:, c], grad.at[c]),
+                "part": (part_ref.at[c], part.at[c]),
+                "right": (right_ref.at[c], right.at[c]),
+            }
+            for name in names:
+                copies[c, name] = pltpu.make_async_copy(*pairs[name], sems.at[len(copies)])
+                copies[c, name].start()
+
+        fetch(0, "left", "grad")
         for c in range(slots):
-            fetch((c, "left"), left_ref.at[c], left.at[c])
-            fetch((c, "grad"), grad_ref.at[:, c], grad.at[c])
-            fetch((c, "part"), part_ref.at[c], part.at[c])
-            fetch((c, "right"), right_ref.at[c], right.at[c])
-        for c in range(slots):
-            for name in ("left", "grad"):
-                copies[c, name].wait()
-            for n, (at, wide) in enumerate(cuts):
-                half[:, done + at : done + at + wide] = jnp.dot(
-                    left[c], grad[c, :, :, at : at + wide].reshape(size, wide), preferred_element_type=F32
-                ).astype(BF16)
-            for name in ("part", "right"):
-                copies[c, name].wait()
+            copies[c, "left"].wait()
+            copies[c, "grad"].wait()
+            fetch(c, "part", "right")
+            half[:, done:] = jnp.dot(
+                left[c], grad[c].reshape(size, width), preferred_element_type=F32
+            ).astype(BF16)
+            copies[c, "part"].wait()
             half[:, :done] = part[c]
+            copies[c, "right"].wait()
+            if c + 1 < slots:
+                fetch(c + 1, "left", "grad")
             for n in range(size // tile):
                 total = jnp.dot(
                     half[...], right[c, :, n * tile : (n + 1) * tile], preferred_element_type=F32
@@ -314,16 +385,18 @@
 def collect_update(places, received):
     owners, slots, rows, col = received.shape
 
-    def body(place_ref, got_ref, out_ref):
+    def body(place_ref, got_ref, out_ref, sem):
         for block in range(NBLOCKS):
-            out_ref[block] = got_ref[place_ref[block]]
-
-    return pl.pallas_call(
-        body,
-        in_specs=[SMEM, VMEM],
+            pltpu.make_async_copy(got_ref.at[place_ref[block]], out_ref.at[block], sem).start()
+        pltpu.make_async_copy(got_ref.at[pl.ds(0, NBLOCKS)], out_ref, sem).wait()
+
+    return pl.pallas_call(
+        body,
+        in_specs=[SMEM, HBM],
         out_specs=VMEM,
         out_shape=shape(NBLOCKS, rows, col),
-        compiler_params=params(16),
+        scratch_shapes=[pltpu.SemaphoreType.DMA],
+        compiler_params=params(59),
         cost_estimate=cost(0, 4 * NBLOCKS * rows * col * 2),
         name="collect_update",
     )(places, received.reshape(owners * slots, rows, col))
@@ -343,9 +416,9 @@
     def along_z(pair):
         return lax.ppermute(pair[0], "z", up), lax.ppermute(pair[1], "z", down)
 
-    blocks, outgoing, outgoing_rest = gather_partner(table, partials)
+    blocks, outgoing = gather_first(table, partials)
     received = lax.ppermute(outgoing, "core", swap)
-    own = gather_own(blocks, partials)
+    *own, outgoing_rest = gather_rest(blocks, partials)
     outgoing_rest, received, own = lax.optimization_barrier((outgoing_rest, received, own))
     received_rest = lax.ppermute(outgoing_rest, "core", swap)
 
@@ -354,18 +427,14 @@
 
     *pair_a, wait_a, stay_a = add_pair(own[0], received, 0)
     got_a = along_z(pair_a)
-    *pair_b, wait_b, stay_b = add_pair(after(own[1], stay_a), received_rest, 0)
-    got_b = along_z(pair_b)
-    late_a = add_waiting(after(wait_a, stay_b), *got_a)
-    *pair_c, wait_c, stay_c = add_pair(after(own[2], late_a[0]), received_rest, SPLITS[1])
-    late_a = along_z(late_a)
-    got_c = along_z(lax.optimization_barrier((*pair_c, *got_b, *late_a)))
-    picked_a = add_last_and_pick(table, [(after(stay_a, stay_c), *got_a, *late_a)])
-    arrived = [lax.all_to_all(picked_a, "owner", split_axis=0, concat_axis=0, tiled=True)]
-    late_b = add_waiting(after(wait_b, picked_a), *got_b)
-    late_c = add_waiting(after(wait_c, late_b[0]), *got_c)
-    late_b, late_c = along_z(late_b), along_z(late_c)
-    picked = add_last_and_pick(table, [(stay_b, *got_b, *late_b), (stay_c, *got_c, *late_c)])
+    *mixed, wait_b, stay_b = mix_first_second(wait_a, *got_a, own[1], received_rest)
+    *pair_c, wait_c, stay_c = add_pair(after(own[2], stay_b), received_rest, SPLITS[1])
+    mixed = along_z(mixed)
+    got_c = along_z(pair_c)
+    picked = last_of_first(table, after(stay_a, stay_c), *got_a, *mixed)
+    arrived = [lax.all_to_all(picked, "owner", split_axis=0, concat_axis=0, tiled=True)]
+    late = along_z(add_waiting(after(wait_b, picked), *mixed, wait_c, *got_c))
+    picked = last_of_rest(table, stay_b, *mixed, stay_c, *got_c, *late)
     arrived.append(lax.all_to_all(picked, "owner", split_axis=0, concat_axis=0, tiled=True))
 
     left_part = left_product(left_root, arrived[0])

time: 183 us -> 178 us (0.973)
  starting transfers between devices: 45.6 us -> 37.6 us
  waiting for transfers between devices: 85.8 us -> 88.9 us
    all_to_all x1 -> x0, starting transfers between devices: 6.77 us -> none  [local(): lax.all_to_all(picked_a, 'owner', split_axis=0, concat_axis=0, tiled=True)]
    all_to_all x1 -> x2, starting transfers between devices: 6.6 us -> 10.8 us  [local(): lax.all_to_all(picked, 'owner', split_axis=0, concat_axis=0, tiled=True)]
    ppermute x12 -> x8, starting transfers between devices: 16.1 us -> 12.2 us  [along_z(): return (lax.ppermute(pair[0], 'z', up), lax.ppermute(pair[1], 'z', down))]
    ppermute x12 -> x8, waiting for transfers between devices: 16.5 us -> 19 us  [along_z(): return (lax.ppermute(pair[0], 'z', up), lax.ppermute(pair[1], 'z', down))]
    all_to_all x1 -> x2, waiting for transfers between devices: 30.6 us -> 32.7 us  [local(): lax.all_to_all(picked, 'owner', split_axis=0, concat_axis=0, tiled=True)]
    unnamed x12 -> x16, local copies, waits for them, and re-layouts: 5.41 us -> 5.98 us
    pallas_call x8 -> x7, Pallas kernels: 14.3 us -> 14.3 us  [the longest x2 4.12 us: last_call(): pl.pallas_call(body, in_specs=[SMEM] + [VMEM] * len(arrays), out_specs=HB...]
  transfers between devices with their start and end apart: 17 -> 13, of which waited for: 8 -> 6; matrix products, arithmetic and copies ran while one was open for 0% -> 0% of each run, Pallas kernels for 13% -> 14%
where the time goes in v2:
time: 178 us
  waiting for transfers between devices  88.9 us (50%)
  Pallas kernels  44.4 us (25%)
  starting transfers between devices  37.6 us (21%)
  local copies, waits for them, and re-layouts  5.98 us (3%)
    all_to_all x1, waiting for transfers between devices, local(): lax.all_to_all(pieces, ('z', 'core', 'owner'), split_axis=0, concat_axis=...  37.2 us
    all_to_all x2, waiting for transfers between devices, local(): lax.all_to_all(picked, 'owner', split_axis=0, concat_axis=0, tiled=True)  32.7 us
    ppermute x8, waiting for transfers between devices, along_z(): return (lax.ppermute(pair[0], 'z', up), lax.ppermute(pair[1], 'z', down))  19 us
    pallas_call x1, Pallas kernels, gram_products(): pl.pallas_call(body, grid=(slots, size // tile), in_specs=[SMEM] + [pl.Bl...  13.8 us
    all_to_all x1, starting transfers between devices, local(): lax.all_to_all(pieces, ('z', 'core', 'owner'), split_axis=0, concat_axis=...  13.1 us
    pallas_call x1, Pallas kernels, finish_update(): pl.pallas_call(body, in_specs=[HBM] * 4, out_specs=HBM, out_shape=shape(s...  12.6 us
    ppermute x8, starting transfers between devices, along_z(): return (lax.ppermute(pair[0], 'z', up), lax.ppermute(pair[1], 'z', down))  12.2 us
    all_to_all x2, starting transfers between devices, local(): lax.all_to_all(picked, 'owner', split_axis=0, concat_axis=0, tiled=True)  10.8 us
  transfers between devices with their start and end apart: 13, of which 6 were waited for; matrix products, arithmetic and copies ran while one was open for 0% of the time, Pallas kernels for 14%

profile of v2, /device:TPU:1, one launch (start us, length us, event | category | flops | bytes accessed | tf_op | source)
XLA Modules:
  0.0 177.9 jit_solution(18391737556985655946)
XLA Ops:
  0.6 0.0 copy-start.4
  0.6 0.7 copy-done.4
  1.3 2.9 %gather_first.1 = (s32[72]{0:T(128)S(1)}, bf16[32,64,256]{2,1,0:T(8,128)(2,1)S(1)}) custom-call(s32[2,128]{1,0:T(2,128)S(1)} %bitcast.10, bf16[64,64,1024]{2,1,0:T(8,128)(2,1)} %bitcast.14), custom_call_target="tpu_custom_call" | custom-call | bytes 2097152 | tf_op jit(solution)/shard_map/gather_first/pallas_call | solution.py:77
  4.2 1.5 collective-permute-start
  5.7 3.8 %gather_rest.1 = (bf16[32,64,256]{2,1,0:T(8,128)(2,1)S(1)}, bf16[32,64,384]{2,1,0:T(8,128)(2,1)S(1)}, bf16[32,64,384]{2,1,0:T(8,128)(2,1)S(1)}, bf16[32,64,768]{2,1,0:T(8,128)(2,1)S(1)}) custom-call(s32[72]{0:T(128)S(1)} %get-tuple-element.37.block_ref, bf16[64,64,1024]{2,1,0:T(8,128)(2,1)} %bitcast.15), custom_call_target="tpu_custom_call" | custom-call | bytes 14680064 | tf_op jit(solution)/shard_map/gather_rest/pallas_call | solution.py:101
  9.5 0.0 collective-permute-done.got_ref
  9.5 0.1 collective-permute-start.3
  9.6 0.2 add_core_pair.2
  9.9 1.8 %collective-permute-start.1 = (bf16[8,64,256]{2,1,0:T(8,128)(2,1)S(1)}, bf16[8,64,256]{2,1,0:T(8,128)(2,1)S(1)}, u32[]{:S(2)}, u32[]{:S(2)}) collective-permute-start(bf16[8,64,256]{2,1,0:T(8,128)(2,1)S(1)} %get-tuple-element.48), channel_id=1, source_target_pairs={{0,32},{32,64},{64,96},{96,0},{1,33},{33,65},{65,97},{97,1},{2,34}... | collective-permute-start | bytes 786440 | tf_op jit(solution)/shard_map/ppermute | solution.py:417
  11.7 2.2 %collective-permute-start.2 = (bf16[8,64,256]{2,1,0:T(8,128)(2,1)S(1)}, bf16[8,64,256]{2,1,0:T(8,128)(2,1)S(1)}, u32[]{:S(2)}, u32[]{:S(2)}) collective-permute-start(bf16[8,64,256]{2,1,0:T(8,128)(2,1)S(1)} %get-tuple-element.49), channel_id=1, source_target_pairs={{0,96},{32,0},{64,32},{96,64},{1,97},{33,1},{65,33},{97,65},{2,98}... | collective-permute-start | bytes 786440 | tf_op jit(solution)/shard_map/ppermute | solution.py:417
  13.9 6.2 %collective-permute-done.1.up_ref = bf16[8,64,256]{2,1,0:T(8,128)(2,1)S(1)} collective-permute-done((bf16[8,64,256]{2,1,0:T(8,128)(2,1)S(1)}, bf16[8,64,256]{2,1,0:T(8,128)(2,1)S(1)}, u32[]{:S(2)}, u32[]{:S(2)}) %collective-permute-start.1) | collective-permute-done | bytes 262176 | tf_op jit(solution)/shard_map/ppermute | solution.py:417
  20.0 0.0 collective-permute-done.2.down_ref
  20.0 0.0 collective-permute-done.3.got_ref
  20.0 0.0 copy-start.5
  20.1 0.5 mix_first_second.1
  20.5 0.4 collective-permute-start.4
  20.9 2.3 %collective-permute-start.5 = (bf16[32,64,128]{2,1,0:T(8,128)(2,1)S(1)}, bf16[32,64,128]{2,1,0:T(8,128)(2,1)S(1)}, u32[]{:S(2)}, u32[]{:S(2)}) collective-permute-start(bf16[32,64,128]{2,1,0:T(8,128)(2,1)S(1)} %get-tuple-element.57), channel_id=1, source_target_pairs={{0,96},{32,0},{64,32},{96,64},{1,97},{33,1},{65,33},{97,65},{2,98}... | collective-permute-start | bytes 1572872 | tf_op jit(solution)/shard_map/ppermute | solution.py:417
  23.3 1.0 add_core_pair.3
  24.2 0.0 collective-permute-start.6
  24.2 2.7 %collective-permute-start.7 = (bf16[8,64,384]{2,1,0:T(8,128)(2,1)}, bf16[8,64,384]{2,1,0:T(8,128)(2,1)S(1)}, u32[]{:S(2)}, u32[]{:S(2)}) collective-permute-start(bf16[8,64,384]{2,1,0:T(8,128)(2,1)} %get-tuple-element.59), channel_id=1, source_target_pairs={{0,96},{32,0},{64,32},{96,64},{1,97},{33,1},{65,33},{97,65},{2,98}... | collective-permute-start | bytes 1179656 | tf_op jit(solution)/shard_map/ppermute | solution.py:417
  26.9 7.3 %collective-permute-done.4.mixed_up_ref = bf16[32,64,128]{2,1,0:T(8,128)(2,1)S(1)} collective-permute-done((bf16[32,64,128]{2,1,0:T(8,128)(2,1)S(1)}, bf16[32,64,128]{2,1,0:T(8,128)(2,1)S(1)}, u32[]{:S(2)}, u32[]{:S(2)}) %collective-permute-start.4) | collective-permute-done | bytes 524320 | tf_op jit(solution)/shard_map/ppermute | solution.py:417
  34.2 0.0 collective-permute-done.5.mixed_down_ref
  34.2 0.0 copy-done.5
  34.2 1.6 add_last_and_pick.2
  35.8 6.8 %all-to-all-start = ((bf16[16,2,64,256]{3,2,1,0:T(8,128)(2,1)}), bf16[16,2,64,256]{3,2,1,0:T(8,128)(2,1)}, u32[]{:S(2)}, u32[]{:S(2)}) async-start(bf16[16,2,64,256]{3,2,1,0:T(8,128)(2,1)} %add_last_and_pick.2), calls=%async_computation | async-start | bytes 2097152 | tf_op jit(solution)/shard_map/all_to_all | solution.py:435
  42.6 0.0 collective-permute-done.6.up_ref
  42.6 0.0 collective-permute-done.7.down_ref
  42.7 0.0 copy-start.6
  42.7 0.2 add_waiting.1
  42.9 0.1 collective-permute-start.8
  43.0 2.7 %collective-permute-start.9 = (bf16[4,64,768]{2,1,0:T(8,128)(2,1)S(1)}, bf16[4,64,768]{2,1,0:T(8,128)(2,1)S(1)}, u32[]{:S(2)}, u32[]{:S(2)}) collective-permute-start(bf16[4,64,768]{2,1,0:T(8,128)(2,1)S(1)} %get-tuple-element.64), channel_id=1, source_target_pairs={{0,96},{32,0},{64,32},{96,64},{1,97},{33,1},{65,33},{97,65},{2,98}... | collective-permute-start | bytes 1179656 | tf_op jit(solution)/shard_map/ppermute | solution.py:417
  45.6 5.6 %collective-permute-done.8.late_up_ref = bf16[4,64,768]{2,1,0:T(8,128)(2,1)S(1)} collective-permute-done((bf16[4,64,768]{2,1,0:T(8,128)(2,1)S(1)}, bf16[4,64,768]{2,1,0:T(8,128)(2,1)S(1)}, u32[]{:S(2)}, u32[]{:S(2)}) %collective-permute-start.8) | collective-permute-done | bytes 393248 | tf_op jit(solution)/shard_map/ppermute | solution.py:417
  51.2 0.0 collective-permute-done.9.late_down_ref
  51.2 0.0 copy-done.6
  51.2 2.5 %add_last_and_pick.3 = bf16[16,2,64,768]{3,2,1,0:T(8,128)(2,1)} custom-call(s32[2,128]{1,0:T(2,128)S(1)} %bitcast.12, bf16[8,64,384]{2,1,0:T(8,128)(2,1)S(1)} %get-tuple-element.52.b_ref, bf16[32,64,128]{2,1,0:T(8,128)(2,1)S(1)} %collective-permute-done.4.mixed_up_ref, bf16[32,64,128]{2,1,0:T(8,128)(2,1)S(1)} %collective-permute-done.5.mixed_down_ref, ...), custom_call_target="tpu_custom_call" | custom-call | bytes 5505024 | tf_op jit(solution)/shard_map/add_last_and_pick/pallas_call | solution.py:201
  53.7 2.6 %all-to-all-done.grad_ref.refs_0_ = bf16[16,2,64,256]{3,2,1,0:T(8,128)(2,1)} async-done(((bf16[16,2,64,256]{3,2,1,0:T(8,128)(2,1)}), bf16[16,2,64,256]{3,2,1,0:T(8,128)(2,1)}, u32[]{:S(2)}, u32[]{:S(2)}) %all-to-all-start) | async-done | bytes 1048608 | tf_op jit(solution)/shard_map/all_to_all | solution.py:435
  56.3 4.0 %all-to-all-start.1 = ((bf16[16,2,64,768]{3,2,1,0:T(8,128)(2,1)}), bf16[16,2,64,768]{3,2,1,0:T(8,128)(2,1)S(1)}, u32[]{:S(2)}, u32[]{:S(2)}) async-start(bf16[16,2,64,768]{3,2,1,0:T(8,128)(2,1)} %add_last_and_pick.3), calls=%async_computation.1 | async-start | bytes 6291456 | tf_op jit(solution)/shard_map/all_to_all | solution.py:438
  60.3 0.0 copy-start
  60.3 2.2 %copy-done = bf16[1,2,1024,1024]{3,2,1,0:T(8,128)(2,1)S(1)} copy-done((bf16[1,2,1024,1024]{3,2,1,0:T(8,128)(2,1)S(1)}, bf16[1,2,1024,1024]{3,2,1,0:T(8,128)(2,1)}, u32[]{:S(2)}) %copy-start) | copy-done | bytes 4194328
  62.5 2.5 %left_product.1.part_ref = bf16[2,1024,256]{2,1,0:T(8,128)(2,1)S(1)} custom-call(bf16[2,1024,1024]{2,1,0:T(8,128)(2,1)S(1)} %bitcast.9, bf16[16,2,64,256]{3,2,1,0:T(8,128)(2,1)} %all-to-all-done.grad_ref.refs_0_), custom_call_target="tpu_custom_call" | custom-call | flops 1073741824 | bytes 6291456 | tf_op jit(solution)/shard_map/left_product/pallas_call | solution.py:257
  65.0 0.0 copy-start.3
  65.0 1.0 copy-done.3
  65.9 30.1 %all-to-all-done.1.grad_ref.refs_1_ = bf16[16,2,64,768]{3,2,1,0:T(8,128)(2,1)S(1)} async-done(((bf16[16,2,64,768]{3,2,1,0:T(8,128)(2,1)}), bf16[16,2,64,768]{3,2,1,0:T(8,128)(2,1)S(1)}, u32[]{:S(2)}, u32[]{:S(2)}) %all-to-all-start.1) | async-done | bytes 3145760 | tf_op jit(solution)/shard_map/all_to_all | solution.py:438
  96.1 0.0 copy-start.1
  96.1 1.7 copy-done.1
  97.7 12.6 %finish_update.1 = bf16[8,16,2,64,128]{4,3,2,1,0:T(8,128)(2,1)} custom-call(bf16[2,1024,1024]{2,1,0:T(8,128)(2,1)} %bitcast.8, bf16[2,1024,1024]{2,1,0:T(8,128)(2,1)} %bitcast.17, bf16[2,1024,256]{2,1,0:T(8,128)(2,1)} %copy-done.3, bf16[16,2,64,768]{3,2,1,0:T(8,128)(2,1)} %copy-done.1), custom_call_target="tpu_custom_call" | custom-call | flops 7516192768 | bytes 12582912 | tf_op jit(solution)/shard_map/finish_update/pallas_call | solution.py:316
  110.3 0.0 copy-start.2
  110.3 13.1 %all-to-all-start.2 = ((bf16[128,2,64,128]{3,2,1,0:T(8,128)(2,1)}), bf16[128,2,64,128]{3,2,1,0:T(8,128)(2,1)}, u32[]{:S(2)}, u32[]{:S(2)}) async-start(bf16[128,2,64,128]{3,2,1,0:T(8,128)(2,1)} %bitcast.16), calls=%async_computation.2 | async-start | bytes 8388608 | tf_op jit(solution)/shard_map/all_to_all | solution.py:444
  123.4 0.0 copy-done.2
  123.4 13.8 %gram_products.1 = (bf16[2,1024,1024]{2,1,0:T(8,128)(2,1)}, bf16[2,1024,1024]{2,1,0:T(8,128)(2,1)}, s32[65]{0:T(128)S(1)}) custom-call(s32[2,128]{1,0:T(2,128)S(1)} %bitcast.13, bf16[16,2,64,256]{3,2,1,0:T(8,128)(2,1)} %all-to-all-done.grad_ref.refs_0_, bf16[16,2,64,768]{3,2,1,0:T(8,128)(2,1)S(1)} %copy-done.2), custom_call_target="tpu_custom_call" | custom-call | flops 8589934592 | bytes 12582912 | tf_op jit(solution)/shard_map/gram_products/pallas_call | solution.py:371
  137.2 0.0 copy-start.7
  137.2 0.5 copy-done.7
  137.7 37.2 %all-to-all-done.2 = bf16[128,2,64,128]{3,2,1,0:T(8,128)(2,1)} async-done(((bf16[128,2,64,128]{3,2,1,0:T(8,128)(2,1)}), bf16[128,2,64,128]{3,2,1,0:T(8,128)(2,1)}, u32[]{:S(2)}, u32[]{:S(2)}) %all-to-all-start.2) | async-done | bytes 4194336 | tf_op jit(solution)/shard_map/all_to_all | solution.py:444
  174.9 2.8 %collect_update.1 = bf16[64,64,128]{2,1,0:T(8,128)(2,1)} custom-call(s32[65]{0:T(128)} %copy-done.7, bf16[256,64,128]{2,1,0:T(8,128)(2,1)} %bitcast.7.got_ref), custom_call_target="tpu_custom_call" | custom-call | bytes 4194304 | tf_op jit(solution)/shard_map/collect_update/pallas_call | solution.py:393
Async XLA Ops:
  0.6 0.7 copy-start.4
  4.2 5.4 %collective-permute-start = (bf16[32,64,256]{2,1,0:T(8,128)(2,1)S(1)}, bf16[32,64,256]{2,1,0:T(8,128)(2,1)S(1)}, u32[]{:S(2)}, u32[]{:S(2)}) collective-permute-start(bf16[32,64,256]{2,1,0:T(8,128)(2,1)S(1)} %get-tuple-element.39), channel_id=1, source_target_pairs={{0,16},{16,0},{1,17},{17,1},{2,18},{18,2},{3,19},{19,3},{4,20},{20... | collective-permute-start | bytes 3145736 | tf_op jit(solution)/shard_map/ppermute | solution.py:420
  9.5 10.5 %collective-permute-start.3 = (bf16[32,64,768]{2,1,0:T(8,128)(2,1)S(1)}, bf16[32,64,768]{2,1,0:T(8,128)(2,1)S(1)}, u32[]{:S(2)}, u32[]{:S(2)}) collective-permute-start(bf16[32,64,768]{2,1,0:T(8,128)(2,1)S(1)} %get-tuple-element.51), channel_id=1, source_target_pairs={{0,16},{16,0},{1,17},{17,1},{2,18},{18,2},{3,19},{19,3},{4,20},{20... | collective-permute-start | bytes 9437192 | tf_op jit(solution)/shard_map/ppermute | solution.py:423
  9.9 10.2 %collective-permute-start.1 = (bf16[8,64,256]{2,1,0:T(8,128)(2,1)S(1)}, bf16[8,64,256]{2,1,0:T(8,128)(2,1)S(1)}, u32[]{:S(2)}, u32[]{:S(2)}) collective-permute-start(bf16[8,64,256]{2,1,0:T(8,128)(2,1)S(1)} %get-tuple-element.48), channel_id=1, source_target_pairs={{0,32},{32,64},{64,96},{96,0},{1,33},{33,65},{65,97},{97,1},{2,34}... | collective-permute-start | bytes 786440 | tf_op jit(solution)/shard_map/ppermute | solution.py:417
  11.7 8.4 %collective-permute-start.2 = (bf16[8,64,256]{2,1,0:T(8,128)(2,1)S(1)}, bf16[8,64,256]{2,1,0:T(8,128)(2,1)S(1)}, u32[]{:S(2)}, u32[]{:S(2)}) collective-permute-start(bf16[8,64,256]{2,1,0:T(8,128)(2,1)S(1)} %get-tuple-element.49), channel_id=1, source_target_pairs={{0,96},{32,0},{64,32},{96,64},{1,97},{33,1},{65,33},{97,65},{2,98}... | collective-permute-start | bytes 786440 | tf_op jit(solution)/shard_map/ppermute | solution.py:417
  20.0 14.1 %copy-start.5 = (s32[128,2]{0,1:T(2,128)S(1)}, s32[128,2]{0,1:T(2,128)}, u32[]{:S(2)}) copy-start(s32[128,2]{0,1:T(2,128)} %param.5) | copy-start | bytes 3076
  20.5 13.7 %collective-permute-start.4 = (bf16[32,64,128]{2,1,0:T(8,128)(2,1)S(1)}, bf16[32,64,128]{2,1,0:T(8,128)(2,1)S(1)}, u32[]{:S(2)}, u32[]{:S(2)}) collective-permute-start(bf16[32,64,128]{2,1,0:T(8,128)(2,1)S(1)} %get-tuple-element.56), channel_id=1, source_target_pairs={{0,32},{32,64},{64,96},{96,0},{1,33},{33,65},{65,97},{97,1},{2,34}... | collective-permute-start | bytes 1572872 | tf_op jit(solution)/shard_map/ppermute | solution.py:417
  20.9 13.3 %collective-permute-start.5 = (bf16[32,64,128]{2,1,0:T(8,128)(2,1)S(1)}, bf16[32,64,128]{2,1,0:T(8,128)(2,1)S(1)}, u32[]{:S(2)}, u32[]{:S(2)}) collective-permute-start(bf16[32,64,128]{2,1,0:T(8,128)(2,1)S(1)} %get-tuple-element.57), channel_id=1, source_target_pairs={{0,96},{32,0},{64,32},{96,64},{1,97},{33,1},{65,33},{97,65},{2,98}... | collective-permute-start | bytes 1572872 | tf_op jit(solution)/shard_map/ppermute | solution.py:417
  24.2 18.4 %collective-permute-start.6 = (bf16[8,64,384]{2,1,0:T(8,128)(2,1)}, bf16[8,64,384]{2,1,0:T(8,128)(2,1)S(1)}, u32[]{:S(2)}, u32[]{:S(2)}) collective-permute-start(bf16[8,64,384]{2,1,0:T(8,128)(2,1)} %get-tuple-element.58), channel_id=1, source_target_pairs={{0,32},{32,64},{64,96},{96,0},{1,33},{33,65},{65,97},{97,1},{2,34}... | collective-permute-start | bytes 1179656 | tf_op jit(solution)/shard_map/ppermute | solution.py:417
  24.2 18.4 %collective-permute-start.7 = (bf16[8,64,384]{2,1,0:T(8,128)(2,1)}, bf16[8,64,384]{2,1,0:T(8,128)(2,1)S(1)}, u32[]{:S(2)}, u32[]{:S(2)}) collective-permute-start(bf16[8,64,384]{2,1,0:T(8,128)(2,1)} %get-tuple-element.59), channel_id=1, source_target_pairs={{0,96},{32,0},{64,32},{96,64},{1,97},{33,1},{65,33},{97,65},{2,98}... | collective-permute-start | bytes 1179656 | tf_op jit(solution)/shard_map/ppermute | solution.py:417
  35.8 20.5 %all-to-all-start = ((bf16[16,2,64,256]{3,2,1,0:T(8,128)(2,1)}), bf16[16,2,64,256]{3,2,1,0:T(8,128)(2,1)}, u32[]{:S(2)}, u32[]{:S(2)}) async-start(bf16[16,2,64,256]{3,2,1,0:T(8,128)(2,1)} %add_last_and_pick.2), calls=%async_computation | async-start | bytes 2097152 | tf_op jit(solution)/shard_map/all_to_all | solution.py:435
  42.7 8.5 %copy-start.6 = (s32[128,2]{0,1:T(2,128)S(1)}, s32[128,2]{0,1:T(2,128)}, u32[]{:S(2)}) copy-start(s32[128,2]{0,1:T(2,128)} %param.5) | copy-start | bytes 3076
  42.9 8.3 %collective-permute-start.8 = (bf16[4,64,768]{2,1,0:T(8,128)(2,1)S(1)}, bf16[4,64,768]{2,1,0:T(8,128)(2,1)S(1)}, u32[]{:S(2)}, u32[]{:S(2)}) collective-permute-start(bf16[4,64,768]{2,1,0:T(8,128)(2,1)S(1)} %get-tuple-element.63), channel_id=1, source_target_pairs={{0,32},{32,64},{64,96},{96,0},{1,33},{33,65},{65,97},{97,1},{2,34}... | collective-permute-start | bytes 1179656 | tf_op jit(solution)/shard_map/ppermute | solution.py:417
  43.0 8.2 %collective-permute-start.9 = (bf16[4,64,768]{2,1,0:T(8,128)(2,1)S(1)}, bf16[4,64,768]{2,1,0:T(8,128)(2,1)S(1)}, u32[]{:S(2)}, u32[]{:S(2)}) collective-permute-start(bf16[4,64,768]{2,1,0:T(8,128)(2,1)S(1)} %get-tuple-element.64), channel_id=1, source_target_pairs={{0,96},{32,0},{64,32},{96,64},{1,97},{33,1},{65,33},{97,65},{2,98}... | collective-permute-start | bytes 1179656 | tf_op jit(solution)/shard_map/ppermute | solution.py:417
  56.3 39.8 %all-to-all-start.1 = ((bf16[16,2,64,768]{3,2,1,0:T(8,128)(2,1)}), bf16[16,2,64,768]{3,2,1,0:T(8,128)(2,1)S(1)}, u32[]{:S(2)}, u32[]{:S(2)}) async-start(bf16[16,2,64,768]{3,2,1,0:T(8,128)(2,1)} %add_last_and_pick.3), calls=%async_computation.1 | async-start | bytes 6291456 | tf_op jit(solution)/shard_map/all_to_all | solution.py:438
  60.3 2.2 %copy-start = (bf16[1,2,1024,1024]{3,2,1,0:T(8,128)(2,1)S(1)}, bf16[1,2,1024,1024]{3,2,1,0:T(8,128)(2,1)}, u32[]{:S(2)}) copy-start(bf16[1,2,1024,1024]{3,2,1,0:T(8,128)(2,1)} %param.6) | copy-start | bytes 12582916
  65.0 1.0 copy-start.3
  96.1 1.7 copy-start.1
  110.3 13.1 %copy-start.2 = (bf16[16,2,64,768]{3,2,1,0:T(8,128)(2,1)S(1)}, bf16[16,2,64,768]{3,2,1,0:T(8,128)(2,1)}, u32[]{:S(2)}) copy-start(bf16[16,2,64,768]{3,2,1,0:T(8,128)(2,1)} %copy-done.1) | copy-start | bytes 9437188
  110.3 64.6 %all-to-all-start.2 = ((bf16[128,2,64,128]{3,2,1,0:T(8,128)(2,1)}), bf16[128,2,64,128]{3,2,1,0:T(8,128)(2,1)}, u32[]{:S(2)}, u32[]{:S(2)}) async-start(bf16[128,2,64,128]{3,2,1,0:T(8,128)(2,1)} %bitcast.16), calls=%async_computation.2 | async-start | bytes 8388608 | tf_op jit(solution)/shard_map/all_to_all | solution.py:444
  137.2 0.5 copy-start.7

commit v3 on v2

--- a/solution.py
+++ b/solution.py
@@ -14,6 +14,7 @@
 VMEM = pl.BlockSpec(memory_space=pltpu.VMEM)
 SMEM = pl.BlockSpec(memory_space=pltpu.SMEM)
 HBM = pl.BlockSpec(memory_space=pltpu.HBM)
+ANY = pl.BlockSpec(memory_space=pl.ANY)
 
 
 def params(mebibytes):
@@ -279,9 +280,12 @@
     def body(left_ref, right_ref, part_ref, grad_ref, out_ref, left, right, part, grad, half, out, sems, out_sem):
         copies = {}
 
+        low, high = slice(0, size // 2), slice(size // 2, size)
+
         def fetch(c, *names):
             pairs = {
-                "left": (left_ref.at[c], left.at[c]),
+                "low": (left_ref.at[c, pl.ds(0, size // 2)], left.at[c, pl.ds(0, size // 2)]),
+                "high": (left_ref.at[c, pl.ds(size // 2, size // 2)], left.at[c, pl.ds(size // 2, size // 2)]),
                 "grad": (grad_ref.at[:, c], grad.at[c]),
                 "part": (part_ref.at[c], part.at[c]),
                 "right": (right_ref.at[c], right.at[c]),
@@ -290,19 +294,21 @@
                 copies[c, name] = pltpu.make_async_copy(*pairs[name], sems.at[len(copies)])
                 copies[c, name].start()
 
-        fetch(0, "left", "grad")
+        fetch(0, "grad", "low", "high")
         for c in range(slots):
-            copies[c, "left"].wait()
             copies[c, "grad"].wait()
-            fetch(c, "part", "right")
-            half[:, done:] = jnp.dot(
-                left[c], grad[c].reshape(size, width), preferred_element_type=F32
-            ).astype(BF16)
+            for name, part_rows in (("low", low), ("high", high)):
+                copies[c, name].wait()
+                if name == "low":
+                    fetch(c, "part", "right")
+                half[part_rows, done:] = jnp.dot(
+                    left[c, part_rows], grad[c].reshape(size, width), preferred_element_type=F32
+                ).astype(BF16)
             copies[c, "part"].wait()
             half[:, :done] = part[c]
             copies[c, "right"].wait()
             if c + 1 < slots:
-                fetch(c + 1, "left", "grad")
+                fetch(c + 1, "grad", "low", "high")
             for n in range(size // tile):
                 total = jnp.dot(
                     half[...], right[c, :, n * tile : (n + 1) * tile], preferred_element_type=F32
@@ -315,7 +321,7 @@
 
     return pl.pallas_call(
         body,
-        in_specs=[HBM] * 4,
+        in_specs=[HBM, HBM, ANY, ANY],
         out_specs=HBM,
         out_shape=shape(size // col, owners, slots, rows, col),
         scratch_shapes=[
@@ -325,7 +331,7 @@
             pltpu.VMEM((slots, owners, rows, width), BF16),
             pltpu.VMEM((size, size), BF16),
             pltpu.VMEM((size // col, owners, slots, rows, col), BF16),
-            pltpu.SemaphoreType.DMA((4 * slots,)),
+            pltpu.SemaphoreType.DMA((5 * slots,)),
             pltpu.SemaphoreType.DMA,
         ],
         compiler_params=params(59),

time: 178 us -> 178 us (level)
  no operation moved by 1% of the time
where the time goes in v3:
time: 178 us
  waiting for transfers between devices  88.9 us (50%)
  Pallas kernels  44.4 us (25%)
  starting transfers between devices  37.6 us (21%)
  local copies, waits for them, and re-layouts  5.98 us (3%)
    all_to_all x1, waiting for transfers between devices, local(): lax.all_to_all(pieces, ('z', 'core', 'owner'), split_axis=0, concat_axis=...  37.2 us
    all_to_all x2, waiting for transfers between devices, local(): lax.all_to_all(picked, 'owner', split_axis=0, concat_axis=0, tiled=True)  32.7 us
    ppermute x8, waiting for transfers between devices, along_z(): return (lax.ppermute(pair[0], 'z', up), lax.ppermute(pair[1], 'z', down))  19 us
    pallas_call x1, Pallas kernels, gram_products(): pl.pallas_call(body, grid=(slots, size // tile), in_specs=[SMEM] + [pl.Bl...  13.8 us
    all_to_all x1, starting transfers between devices, local(): lax.all_to_all(pieces, ('z', 'core', 'owner'), split_axis=0, concat_axis=...  13.1 us
    pallas_call x1, Pallas kernels, finish_update(): pl.pallas_call(body, in_specs=[HBM, HBM, ANY, ANY], out_specs=HBM, out_sh...  12.5 us
    ppermute x8, starting transfers between devices, along_z(): return (lax.ppermute(pair[0], 'z', up), lax.ppermute(pair[1], 'z', down))  12.2 us
    all_to_all x2, starting transfers between devices, local(): lax.all_to_all(picked, 'owner', split_axis=0, concat_axis=0, tiled=True)  10.8 us
  transfers between devices with their start and end apart: 13, of which 6 were waited for; matrix products, arithmetic and copies ran while one was open for 0% of the time, Pallas kernels for 14%

profile of v3, /device:TPU:1, one launch (start us, length us, event | category | flops | bytes accessed | tf_op | source)
XLA Modules:
  0.0 177.9 jit_solution(876576449276005378)
XLA Ops:
  0.6 0.0 copy-start.4
  0.6 0.7 copy-done.4
  1.3 2.9 %gather_first.1 = (s32[72]{0:T(128)S(1)}, bf16[32,64,256]{2,1,0:T(8,128)(2,1)S(1)}) custom-call(s32[2,128]{1,0:T(2,128)S(1)} %bitcast.10, bf16[64,64,1024]{2,1,0:T(8,128)(2,1)} %bitcast.14), custom_call_target="tpu_custom_call" | custom-call | bytes 2097152 | tf_op jit(solution)/shard_map/gather_first/pallas_call | solution.py:78
  4.2 1.5 collective-permute-start
  5.7 3.8 %gather_rest.1 = (bf16[32,64,256]{2,1,0:T(8,128)(2,1)S(1)}, bf16[32,64,384]{2,1,0:T(8,128)(2,1)S(1)}, bf16[32,64,384]{2,1,0:T(8,128)(2,1)S(1)}, bf16[32,64,768]{2,1,0:T(8,128)(2,1)S(1)}) custom-call(s32[72]{0:T(128)S(1)} %get-tuple-element.37.block_ref, bf16[64,64,1024]{2,1,0:T(8,128)(2,1)} %bitcast.15), custom_call_target="tpu_custom_call" | custom-call | bytes 14680064 | tf_op jit(solution)/shard_map/gather_rest/pallas_call | solution.py:102
  9.5 0.0 collective-permute-done.got_ref
  9.5 0.1 collective-permute-start.3
  9.6 0.2 add_core_pair.2
  9.9 1.8 %collective-permute-start.1 = (bf16[8,64,256]{2,1,0:T(8,128)(2,1)S(1)}, bf16[8,64,256]{2,1,0:T(8,128)(2,1)S(1)}, u32[]{:S(2)}, u32[]{:S(2)}) collective-permute-start(bf16[8,64,256]{2,1,0:T(8,128)(2,1)S(1)} %get-tuple-element.48), channel_id=1, source_target_pairs={{0,32},{32,64},{64,96},{96,0},{1,33},{33,65},{65,97},{97,1},{2,34}... | collective-permute-start | bytes 786440 | tf_op jit(solution)/shard_map/ppermute | solution.py:423
  11.7 2.2 %collective-permute-start.2 = (bf16[8,64,256]{2,1,0:T(8,128)(2,1)S(1)}, bf16[8,64,256]{2,1,0:T(8,128)(2,1)S(1)}, u32[]{:S(2)}, u32[]{:S(2)}) collective-permute-start(bf16[8,64,256]{2,1,0:T(8,128)(2,1)S(1)} %get-tuple-element.49), channel_id=1, source_target_pairs={{0,96},{32,0},{64,32},{96,64},{1,97},{33,1},{65,33},{97,65},{2,98}... | collective-permute-start | bytes 786440 | tf_op jit(solution)/shard_map/ppermute | solution.py:423
  13.9 6.2 %collective-permute-done.1.up_ref = bf16[8,64,256]{2,1,0:T(8,128)(2,1)S(1)} collective-permute-done((bf16[8,64,256]{2,1,0:T(8,128)(2,1)S(1)}, bf16[8,64,256]{2,1,0:T(8,128)(2,1)S(1)}, u32[]{:S(2)}, u32[]{:S(2)}) %collective-permute-start.1) | collective-permute-done | bytes 262176 | tf_op jit(solution)/shard_map/ppermute | solution.py:423
  20.0 0.0 collective-permute-done.2.down_ref
  20.0 0.0 collective-permute-done.3.got_ref
  20.0 0.0 copy-start.5
  20.1 0.5 mix_first_second.1
  20.5 0.4 collective-permute-start.4
  20.9 2.3 %collective-permute-start.5 = (bf16[32,64,128]{2,1,0:T(8,128)(2,1)S(1)}, bf16[32,64,128]{2,1,0:T(8,128)(2,1)S(1)}, u32[]{:S(2)}, u32[]{:S(2)}) collective-permute-start(bf16[32,64,128]{2,1,0:T(8,128)(2,1)S(1)} %get-tuple-element.57), channel_id=1, source_target_pairs={{0,96},{32,0},{64,32},{96,64},{1,97},{33,1},{65,33},{97,65},{2,98}... | collective-permute-start | bytes 1572872 | tf_op jit(solution)/shard_map/ppermute | solution.py:423
  23.3 1.0 add_core_pair.3
  24.2 0.0 collective-permute-start.6
  24.2 2.7 %collective-permute-start.7 = (bf16[8,64,384]{2,1,0:T(8,128)(2,1)}, bf16[8,64,384]{2,1,0:T(8,128)(2,1)S(1)}, u32[]{:S(2)}, u32[]{:S(2)}) collective-permute-start(bf16[8,64,384]{2,1,0:T(8,128)(2,1)} %get-tuple-element.59), channel_id=1, source_target_pairs={{0,96},{32,0},{64,32},{96,64},{1,97},{33,1},{65,33},{97,65},{2,98}... | collective-permute-start | bytes 1179656 | tf_op jit(solution)/shard_map/ppermute | solution.py:423
  26.9 7.3 %collective-permute-done.4.mixed_up_ref = bf16[32,64,128]{2,1,0:T(8,128)(2,1)S(1)} collective-permute-done((bf16[32,64,128]{2,1,0:T(8,128)(2,1)S(1)}, bf16[32,64,128]{2,1,0:T(8,128)(2,1)S(1)}, u32[]{:S(2)}, u32[]{:S(2)}) %collective-permute-start.4) | collective-permute-done | bytes 524320 | tf_op jit(solution)/shard_map/ppermute | solution.py:423
  34.2 0.0 collective-permute-done.5.mixed_down_ref
  34.2 0.0 copy-done.5
  34.2 1.6 add_last_and_pick.2
  35.8 6.8 %all-to-all-start = ((bf16[16,2,64,256]{3,2,1,0:T(8,128)(2,1)}), bf16[16,2,64,256]{3,2,1,0:T(8,128)(2,1)}, u32[]{:S(2)}, u32[]{:S(2)}) async-start(bf16[16,2,64,256]{3,2,1,0:T(8,128)(2,1)} %add_last_and_pick.2), calls=%async_computation | async-start | bytes 2097152 | tf_op jit(solution)/shard_map/all_to_all | solution.py:441
  42.6 0.0 collective-permute-done.6.up_ref
  42.6 0.0 collective-permute-done.7.down_ref
  42.7 0.0 copy-start.6
  42.7 0.2 add_waiting.1
  42.9 0.1 collective-permute-start.8
  43.0 2.7 %collective-permute-start.9 = (bf16[4,64,768]{2,1,0:T(8,128)(2,1)S(1)}, bf16[4,64,768]{2,1,0:T(8,128)(2,1)S(1)}, u32[]{:S(2)}, u32[]{:S(2)}) collective-permute-start(bf16[4,64,768]{2,1,0:T(8,128)(2,1)S(1)} %get-tuple-element.64), channel_id=1, source_target_pairs={{0,96},{32,0},{64,32},{96,64},{1,97},{33,1},{65,33},{97,65},{2,98}... | collective-permute-start | bytes 1179656 | tf_op jit(solution)/shard_map/ppermute | solution.py:423
  45.6 5.6 %collective-permute-done.8.late_up_ref = bf16[4,64,768]{2,1,0:T(8,128)(2,1)S(1)} collective-permute-done((bf16[4,64,768]{2,1,0:T(8,128)(2,1)S(1)}, bf16[4,64,768]{2,1,0:T(8,128)(2,1)S(1)}, u32[]{:S(2)}, u32[]{:S(2)}) %collective-permute-start.8) | collective-permute-done | bytes 393248 | tf_op jit(solution)/shard_map/ppermute | solution.py:423
  51.2 0.0 collective-permute-done.9.late_down_ref
  51.2 0.0 copy-done.6
  51.2 2.5 %add_last_and_pick.3 = bf16[16,2,64,768]{3,2,1,0:T(8,128)(2,1)} custom-call(s32[2,128]{1,0:T(2,128)S(1)} %bitcast.12, bf16[8,64,384]{2,1,0:T(8,128)(2,1)S(1)} %get-tuple-element.52.b_ref, bf16[32,64,128]{2,1,0:T(8,128)(2,1)S(1)} %collective-permute-done.4.mixed_up_ref, bf16[32,64,128]{2,1,0:T(8,128)(2,1)S(1)} %collective-permute-done.5.mixed_down_ref, ...), custom_call_target="tpu_custom_call" | custom-call | bytes 5505024 | tf_op jit(solution)/shard_map/add_last_and_pick/pallas_call | solution.py:202
  53.7 2.6 %all-to-all-done.grad_ref.refs_0_ = bf16[16,2,64,256]{3,2,1,0:T(8,128)(2,1)} async-done(((bf16[16,2,64,256]{3,2,1,0:T(8,128)(2,1)}), bf16[16,2,64,256]{3,2,1,0:T(8,128)(2,1)}, u32[]{:S(2)}, u32[]{:S(2)}) %all-to-all-start) | async-done | bytes 1048608 | tf_op jit(solution)/shard_map/all_to_all | solution.py:441
  56.3 4.0 %all-to-all-start.1 = ((bf16[16,2,64,768]{3,2,1,0:T(8,128)(2,1)}), bf16[16,2,64,768]{3,2,1,0:T(8,128)(2,1)S(1)}, u32[]{:S(2)}, u32[]{:S(2)}) async-start(bf16[16,2,64,768]{3,2,1,0:T(8,128)(2,1)} %add_last_and_pick.3), calls=%async_computation.1 | async-start | bytes 6291456 | tf_op jit(solution)/shard_map/all_to_all | solution.py:444
  60.3 0.0 copy-start
  60.3 2.2 %copy-done = bf16[1,2,1024,1024]{3,2,1,0:T(8,128)(2,1)S(1)} copy-done((bf16[1,2,1024,1024]{3,2,1,0:T(8,128)(2,1)S(1)}, bf16[1,2,1024,1024]{3,2,1,0:T(8,128)(2,1)}, u32[]{:S(2)}) %copy-start) | copy-done | bytes 4194328
  62.5 2.5 %left_product.1.part_ref = bf16[2,1024,256]{2,1,0:T(8,128)(2,1)S(1)} custom-call(bf16[2,1024,1024]{2,1,0:T(8,128)(2,1)S(1)} %bitcast.9, bf16[16,2,64,256]{3,2,1,0:T(8,128)(2,1)} %all-to-all-done.grad_ref.refs_0_), custom_call_target="tpu_custom_call" | custom-call | flops 1073741824 | bytes 6291456 | tf_op jit(solution)/shard_map/left_product/pallas_call | solution.py:258
  65.0 0.0 copy-start.3
  65.0 1.0 copy-done.3
  65.9 30.1 %all-to-all-done.1.grad_ref.refs_1_ = bf16[16,2,64,768]{3,2,1,0:T(8,128)(2,1)S(1)} async-done(((bf16[16,2,64,768]{3,2,1,0:T(8,128)(2,1)}), bf16[16,2,64,768]{3,2,1,0:T(8,128)(2,1)S(1)}, u32[]{:S(2)}, u32[]{:S(2)}) %all-to-all-start.1) | async-done | bytes 3145760 | tf_op jit(solution)/shard_map/all_to_all | solution.py:444
  96.1 0.0 copy-start.1
  96.1 1.7 copy-done.1
  97.7 12.5 %finish_update.1 = bf16[8,16,2,64,128]{4,3,2,1,0:T(8,128)(2,1)} custom-call(bf16[2,1024,1024]{2,1,0:T(8,128)(2,1)} %bitcast.8, bf16[2,1024,1024]{2,1,0:T(8,128)(2,1)} %bitcast.17, bf16[2,1024,256]{2,1,0:T(8,128)(2,1)} %copy-done.3, bf16[16,2,64,768]{3,2,1,0:T(8,128)(2,1)} %copy-done.1), custom_call_target="tpu_custom_call" | custom-call | flops 7516192768 | bytes 12582912 | tf_op jit(solution)/shard_map/finish_update/pallas_call | solution.py:322
  110.3 0.0 copy-start.2
  110.3 13.1 %all-to-all-start.2 = ((bf16[128,2,64,128]{3,2,1,0:T(8,128)(2,1)}), bf16[128,2,64,128]{3,2,1,0:T(8,128)(2,1)}, u32[]{:S(2)}, u32[]{:S(2)}) async-start(bf16[128,2,64,128]{3,2,1,0:T(8,128)(2,1)} %bitcast.16), calls=%async_computation.2 | async-start | bytes 8388608 | tf_op jit(solution)/shard_map/all_to_all | solution.py:450
  123.4 0.0 copy-done.2
  123.4 13.8 %gram_products.1 = (bf16[2,1024,1024]{2,1,0:T(8,128)(2,1)}, bf16[2,1024,1024]{2,1,0:T(8,128)(2,1)}, s32[65]{0:T(128)S(1)}) custom-call(s32[2,128]{1,0:T(2,128)S(1)} %bitcast.13, bf16[16,2,64,256]{3,2,1,0:T(8,128)(2,1)} %all-to-all-done.grad_ref.refs_0_, bf16[16,2,64,768]{3,2,1,0:T(8,128)(2,1)S(1)} %copy-done.2), custom_call_target="tpu_custom_call" | custom-call | flops 8589934592 | bytes 12582912 | tf_op jit(solution)/shard_map/gram_products/pallas_call | solution.py:377
  137.2 0.0 copy-start.7
  137.2 0.5 copy-done.7
  137.6 37.2 %all-to-all-done.2 = bf16[128,2,64,128]{3,2,1,0:T(8,128)(2,1)} async-done(((bf16[128,2,64,128]{3,2,1,0:T(8,128)(2,1)}), bf16[128,2,64,128]{3,2,1,0:T(8,128)(2,1)}, u32[]{:S(2)}, u32[]{:S(2)}) %all-to-all-start.2) | async-done | bytes 4194336 | tf_op jit(solution)/shard_map/all_to_all | solution.py:450
  174.9 2.8 %collect_update.1 = bf16[64,64,128]{2,1,0:T(8,128)(2,1)} custom-call(s32[65]{0:T(128)} %copy-done.7, bf16[256,64,128]{2,1,0:T(8,128)(2,1)} %bitcast.7.got_ref), custom_call_target="tpu_custom_call" | custom-call | bytes 4194304 | tf_op jit(solution)/shard_map/collect_update/pallas_call | solution.py:399
Async XLA Ops:
  0.6 0.7 copy-start.4
  4.2 5.4 %collective-permute-start = (bf16[32,64,256]{2,1,0:T(8,128)(2,1)S(1)}, bf16[32,64,256]{2,1,0:T(8,128)(2,1)S(1)}, u32[]{:S(2)}, u32[]{:S(2)}) collective-permute-start(bf16[32,64,256]{2,1,0:T(8,128)(2,1)S(1)} %get-tuple-element.39), channel_id=1, source_target_pairs={{0,16},{16,0},{1,17},{17,1},{2,18},{18,2},{3,19},{19,3},{4,20},{20... | collective-permute-start | bytes 3145736 | tf_op jit(solution)/shard_map/ppermute | solution.py:426
  9.5 10.5 %collective-permute-start.3 = (bf16[32,64,768]{2,1,0:T(8,128)(2,1)S(1)}, bf16[32,64,768]{2,1,0:T(8,128)(2,1)S(1)}, u32[]{:S(2)}, u32[]{:S(2)}) collective-permute-start(bf16[32,64,768]{2,1,0:T(8,128)(2,1)S(1)} %get-tuple-element.51), channel_id=1, source_target_pairs={{0,16},{16,0},{1,17},{17,1},{2,18},{18,2},{3,19},{19,3},{4,20},{20... | collective-permute-start | bytes 9437192 | tf_op jit(solution)/shard_map/ppermute | solution.py:429
  9.9 10.2 %collective-permute-start.1 = (bf16[8,64,256]{2,1,0:T(8,128)(2,1)S(1)}, bf16[8,64,256]{2,1,0:T(8,128)(2,1)S(1)}, u32[]{:S(2)}, u32[]{:S(2)}) collective-permute-start(bf16[8,64,256]{2,1,0:T(8,128)(2,1)S(1)} %get-tuple-element.48), channel_id=1, source_target_pairs={{0,32},{32,64},{64,96},{96,0},{1,33},{33,65},{65,97},{97,1},{2,34}... | collective-permute-start | bytes 786440 | tf_op jit(solution)/shard_map/ppermute | solution.py:423
  11.7 8.4 %collective-permute-start.2 = (bf16[8,64,256]{2,1,0:T(8,128)(2,1)S(1)}, bf16[8,64,256]{2,1,0:T(8,128)(2,1)S(1)}, u32[]{:S(2)}, u32[]{:S(2)}) collective-permute-start(bf16[8,64,256]{2,1,0:T(8,128)(2,1)S(1)} %get-tuple-element.49), channel_id=1, source_target_pairs={{0,96},{32,0},{64,32},{96,64},{1,97},{33,1},{65,33},{97,65},{2,98}... | collective-permute-start | bytes 786440 | tf_op jit(solution)/shard_map/ppermute | solution.py:423
  20.0 14.1 %copy-start.5 = (s32[128,2]{0,1:T(2,128)S(1)}, s32[128,2]{0,1:T(2,128)}, u32[]{:S(2)}) copy-start(s32[128,2]{0,1:T(2,128)} %param.5) | copy-start | bytes 3076
  20.5 13.7 %collective-permute-start.4 = (bf16[32,64,128]{2,1,0:T(8,128)(2,1)S(1)}, bf16[32,64,128]{2,1,0:T(8,128)(2,1)S(1)}, u32[]{:S(2)}, u32[]{:S(2)}) collective-permute-start(bf16[32,64,128]{2,1,0:T(8,128)(2,1)S(1)} %get-tuple-element.56), channel_id=1, source_target_pairs={{0,32},{32,64},{64,96},{96,0},{1,33},{33,65},{65,97},{97,1},{2,34}... | collective-permute-start | bytes 1572872 | tf_op jit(solution)/shard_map/ppermute | solution.py:423
  20.9 13.3 %collective-permute-start.5 = (bf16[32,64,128]{2,1,0:T(8,128)(2,1)S(1)}, bf16[32,64,128]{2,1,0:T(8,128)(2,1)S(1)}, u32[]{:S(2)}, u32[]{:S(2)}) collective-permute-start(bf16[32,64,128]{2,1,0:T(8,128)(2,1)S(1)} %get-tuple-element.57), channel_id=1, source_target_pairs={{0,96},{32,0},{64,32},{96,64},{1,97},{33,1},{65,33},{97,65},{2,98}... | collective-permute-start | bytes 1572872 | tf_op jit(solution)/shard_map/ppermute | solution.py:423
  24.2 18.4 %collective-permute-start.6 = (bf16[8,64,384]{2,1,0:T(8,128)(2,1)}, bf16[8,64,384]{2,1,0:T(8,128)(2,1)S(1)}, u32[]{:S(2)}, u32[]{:S(2)}) collective-permute-start(bf16[8,64,384]{2,1,0:T(8,128)(2,1)} %get-tuple-element.58), channel_id=1, source_target_pairs={{0,32},{32,64},{64,96},{96,0},{1,33},{33,65},{65,97},{97,1},{2,34}... | collective-permute-start | bytes 1179656 | tf_op jit(solution)/shard_map/ppermute | solution.py:423
  24.2 18.4 %collective-permute-start.7 = (bf16[8,64,384]{2,1,0:T(8,128)(2,1)}, bf16[8,64,384]{2,1,0:T(8,128)(2,1)S(1)}, u32[]{:S(2)}, u32[]{:S(2)}) collective-permute-start(bf16[8,64,384]{2,1,0:T(8,128)(2,1)} %get-tuple-element.59), channel_id=1, source_target_pairs={{0,96},{32,0},{64,32},{96,64},{1,97},{33,1},{65,33},{97,65},{2,98}... | collective-permute-start | bytes 1179656 | tf_op jit(solution)/shard_map/ppermute | solution.py:423
  35.8 20.5 %all-to-all-start = ((bf16[16,2,64,256]{3,2,1,0:T(8,128)(2,1)}), bf16[16,2,64,256]{3,2,1,0:T(8,128)(2,1)}, u32[]{:S(2)}, u32[]{:S(2)}) async-start(bf16[16,2,64,256]{3,2,1,0:T(8,128)(2,1)} %add_last_and_pick.2), calls=%async_computation | async-start | bytes 2097152 | tf_op jit(solution)/shard_map/all_to_all | solution.py:441
  42.7 8.5 %copy-start.6 = (s32[128,2]{0,1:T(2,128)S(1)}, s32[128,2]{0,1:T(2,128)}, u32[]{:S(2)}) copy-start(s32[128,2]{0,1:T(2,128)} %param.5) | copy-start | bytes 3076
  42.9 8.3 %collective-permute-start.8 = (bf16[4,64,768]{2,1,0:T(8,128)(2,1)S(1)}, bf16[4,64,768]{2,1,0:T(8,128)(2,1)S(1)}, u32[]{:S(2)}, u32[]{:S(2)}) collective-permute-start(bf16[4,64,768]{2,1,0:T(8,128)(2,1)S(1)} %get-tuple-element.63), channel_id=1, source_target_pairs={{0,32},{32,64},{64,96},{96,0},{1,33},{33,65},{65,97},{97,1},{2,34}... | collective-permute-start | bytes 1179656 | tf_op jit(solution)/shard_map/ppermute | solution.py:423
  43.0 8.2 %collective-permute-start.9 = (bf16[4,64,768]{2,1,0:T(8,128)(2,1)S(1)}, bf16[4,64,768]{2,1,0:T(8,128)(2,1)S(1)}, u32[]{:S(2)}, u32[]{:S(2)}) collective-permute-start(bf16[4,64,768]{2,1,0:T(8,128)(2,1)S(1)} %get-tuple-element.64), channel_id=1, source_target_pairs={{0,96},{32,0},{64,32},{96,64},{1,97},{33,1},{65,33},{97,65},{2,98}... | collective-permute-start | bytes 1179656 | tf_op jit(solution)/shard_map/ppermute | solution.py:423
  56.3 39.8 %all-to-all-start.1 = ((bf16[16,2,64,768]{3,2,1,0:T(8,128)(2,1)}), bf16[16,2,64,768]{3,2,1,0:T(8,128)(2,1)S(1)}, u32[]{:S(2)}, u32[]{:S(2)}) async-start(bf16[16,2,64,768]{3,2,1,0:T(8,128)(2,1)} %add_last_and_pick.3), calls=%async_computation.1 | async-start | bytes 6291456 | tf_op jit(solution)/shard_map/all_to_all | solution.py:444
  60.3 2.2 %copy-start = (bf16[1,2,1024,1024]{3,2,1,0:T(8,128)(2,1)S(1)}, bf16[1,2,1024,1024]{3,2,1,0:T(8,128)(2,1)}, u32[]{:S(2)}) copy-start(bf16[1,2,1024,1024]{3,2,1,0:T(8,128)(2,1)} %param.6) | copy-start | bytes 12582916
  65.0 1.0 copy-start.3
  96.1 1.7 copy-start.1
  110.3 13.1 %copy-start.2 = (bf16[16,2,64,768]{3,2,1,0:T(8,128)(2,1)S(1)}, bf16[16,2,64,768]{3,2,1,0:T(8,128)(2,1)}, u32[]{:S(2)}) copy-start(bf16[16,2,64,768]{3,2,1,0:T(8,128)(2,1)} %copy-done.1) | copy-start | bytes 9437188
  110.3 64.6 %all-to-all-start.2 = ((bf16[128,2,64,128]{3,2,1,0:T(8,128)(2,1)}), bf16[128,2,64,128]{3,2,1,0:T(8,128)(2,1)}, u32[]{:S(2)}, u32[]{:S(2)}) async-start(bf16[128,2,64,128]{3,2,1,0:T(8,128)(2,1)} %bitcast.16), calls=%async_computation.2 | async-start | bytes 8388608 | tf_op jit(solution)/shard_map/all_to_all | solution.py:450
  137.2 0.5 copy-start.7

commit v4 on v2

--- a/solution.py
+++ b/solution.py
@@ -5,7 +5,7 @@
 from jax.experimental.pallas import tpu as pltpu
 from jax.sharding import Mesh, PartitionSpec as P
 
-SPLITS = (256, 384, 384)
+SPLITS = (256, 256, 512)
 TILE = 128
 GROUPS = 8
 NBLOCKS = 64
@@ -197,7 +197,7 @@
     pltpu.make_async_copy(out_ref, out_ref, sem).wait()
 
 
-def last_call(body, owner_blocks, arrays, rows, width):
+def last_call(body, owner_blocks, arrays, rows, width, estimate):
     return pl.pallas_call(
         body,
         in_specs=[SMEM] + [VMEM] * len(arrays),
@@ -205,7 +205,7 @@
         out_shape=shape(16, 2, rows, width),
         scratch_shapes=[pltpu.VMEM((8, rows, width), BF16), pltpu.SemaphoreType.DMA],
         compiler_params=params(16),
-        cost_estimate=cost(0, 56 * rows * width * 2),
+        cost_estimate=estimate,
         name="add_last_and_pick",
     )(owner_blocks, *arrays)
 
@@ -222,7 +222,8 @@
                 total[4 + t, :, at] = add(own_ref[4 + t, :, at], mixed_down_ref[late * t + n], up_ref[4 + t, :, at])
         pick_slots(table_ref, total, out_ref, sem)
 
-    return last_call(body, owner_blocks, (stay, got_up, got_down, mixed_up, mixed_down), rows, width)
+    estimate = cost(2 * 10**10, 10**8)
+    return last_call(body, owner_blocks, (stay, got_up, got_down, mixed_up, mixed_down), rows, width, estimate)
 
 
 def last_of_rest(owner_blocks, stay_b, mixed_up, mixed_down, stay_c, got_up, got_down, late_up, late_down):
@@ -243,7 +244,7 @@
         pick_slots(table_ref, total, out_ref, sem)
 
     arrays = (stay_b, mixed_up, mixed_down, stay_c, got_up, got_down, late_up, late_down)
-    return last_call(body, owner_blocks, arrays, rows, width)
+    return last_call(body, owner_blocks, arrays, rows, width, cost(0, 56 * rows * width * 2))
 
 
 def left_product(left_root, arrived):

time: 178 us -> 181 us (1.017)
  waiting for transfers between devices: 88.9 us -> 91.4 us
    all_to_all x1, starting transfers between devices: 13.1 us -> 10.2 us  [local(): lax.all_to_all(pieces, ('z', 'core', 'owner'), split_axis=0, concat_axis=...]
    all_to_all x2, starting transfers between devices: 10.8 us -> 13.5 us  [local(): lax.all_to_all(picked, 'owner', split_axis=0, concat_axis=0, tiled=True)]
where the time goes in v4:
time: 181 us; the launch traced here: 180 us
  waiting for transfers between devices  91.4 us (50%)
  Pallas kernels  44.3 us (24%)
  starting transfers between devices  37.4 us (21%)
  local copies, waits for them, and re-layouts  5.98 us (3%)
    all_to_all x1, waiting for transfers between devices, local(): lax.all_to_all(pieces, ('z', 'core', 'owner'), split_axis=0, concat_axis=...  37.2 us
    all_to_all x2, waiting for transfers between devices, local(): lax.all_to_all(picked, 'owner', split_axis=0, concat_axis=0, tiled=True)  33.5 us
    ppermute x8, waiting for transfers between devices, along_z(): return (lax.ppermute(pair[0], 'z', up), lax.ppermute(pair[1], 'z', down))  20.6 us
    pallas_call x1, Pallas kernels, gram_products(): pl.pallas_call(body, grid=(slots, size // tile), in_specs=[SMEM] + [pl.Bl...  13.8 us
    all_to_all x2, starting transfers between devices, local(): lax.all_to_all(picked, 'owner', split_axis=0, concat_axis=0, tiled=True)  13.5 us
    pallas_call x1, Pallas kernels, finish_update(): pl.pallas_call(body, in_specs=[HBM] * 4, out_specs=HBM, out_shape=shape(s...  12.6 us
    ppermute x8, starting transfers between devices, along_z(): return (lax.ppermute(pair[0], 'z', up), lax.ppermute(pair[1], 'z', down))  12.2 us
    all_to_all x1, starting transfers between devices, local(): lax.all_to_all(pieces, ('z', 'core', 'owner'), split_axis=0, concat_axis=...  10.2 us
  transfers between devices with their start and end apart: 13, of which 6 were waited for; matrix products, arithmetic and copies ran while one was open for 0% of the time, Pallas kernels for 14%

profile of v4, /device:TPU:1, one launch (start us, length us, event | category | flops | bytes accessed | tf_op | source)
XLA Modules:
  0.0 180.0 jit_solution(14981626337577919482)
XLA Ops:
  0.6 0.0 copy-start.4
  0.6 0.7 copy-done.4
  1.3 2.9 %gather_first.1 = (s32[72]{0:T(128)S(1)}, bf16[32,64,256]{2,1,0:T(8,128)(2,1)S(1)}) custom-call(s32[2,128]{1,0:T(2,128)S(1)} %bitcast.10, bf16[64,64,1024]{2,1,0:T(8,128)(2,1)} %bitcast.14), custom_call_target="tpu_custom_call" | custom-call | bytes 2097152 | tf_op jit(solution)/shard_map/gather_first/pallas_call | solution.py:77
  4.2 1.5 collective-permute-start
  5.7 3.8 %gather_rest.1 = (bf16[32,64,256]{2,1,0:T(8,128)(2,1)S(1)}, bf16[32,64,256]{2,1,0:T(8,128)(2,1)S(1)}, bf16[32,64,512]{2,1,0:T(8,128)(2,1)S(1)}, bf16[32,64,768]{2,1,0:T(8,128)(2,1)S(1)}) custom-call(s32[72]{0:T(128)S(1)} %get-tuple-element.37.block_ref, bf16[64,64,1024]{2,1,0:T(8,128)(2,1)} %bitcast.15), custom_call_target="tpu_custom_call" | custom-call | bytes 14680064 | tf_op jit(solution)/shard_map/gather_rest/pallas_call | solution.py:101
  9.5 0.0 collective-permute-done.got_ref
  9.5 0.1 collective-permute-start.3
  9.6 0.2 add_core_pair.2
  9.9 1.8 collective-permute-start.1
  11.6 2.2 %collective-permute-start.2 = (bf16[8,64,256]{2,1,0:T(8,128)(2,1)S(1)}, bf16[8,64,256]{2,1,0:T(8,128)(2,1)S(1)}, u32[]{:S(2)}, u32[]{:S(2)}) collective-permute-start(bf16[8,64,256]{2,1,0:T(8,128)(2,1)S(1)} %get-tuple-element.49), channel_id=1, source_target_pairs={{0,96},{32,0},{64,32},{96,64},{1,97},{33,1},{65,33},{97,65},{2,98}... | collective-permute-start | bytes 786440 | tf_op jit(solution)/shard_map/ppermute | solution.py:418
  13.8 6.2 %collective-permute-done.1.up_ref = bf16[8,64,256]{2,1,0:T(8,128)(2,1)S(1)} collective-permute-done((bf16[8,64,256]{2,1,0:T(8,128)(2,1)S(1)}, bf16[8,64,256]{2,1,0:T(8,128)(2,1)S(1)}, u32[]{:S(2)}, u32[]{:S(2)}) %collective-permute-start.1) | collective-permute-done | bytes 262176 | tf_op jit(solution)/shard_map/ppermute | solution.py:418
  20.0 0.0 collective-permute-done.2.down_ref
  20.0 0.0 collective-permute-done.3.got_ref
  20.0 0.0 copy-start.5
  20.0 0.3 mix_first_second.1
  20.3 0.4 collective-permute-start.4
  20.7 2.3 %collective-permute-start.5 = (bf16[24,64,128]{2,1,0:T(8,128)(2,1)S(1)}, bf16[24,64,128]{2,1,0:T(8,128)(2,1)S(1)}, u32[]{:S(2)}, u32[]{:S(2)}) collective-permute-start(bf16[24,64,128]{2,1,0:T(8,128)(2,1)S(1)} %get-tuple-element.57), channel_id=1, source_target_pairs={{0,96},{32,0},{64,32},{96,64},{1,97},{33,1},{65,33},{97,65},{2,98}... | collective-permute-start | bytes 1179656 | tf_op jit(solution)/shard_map/ppermute | solution.py:418
  23.1 1.1 add_core_pair.3
  24.2 0.0 collective-permute-start.6
  24.2 2.7 %collective-permute-start.7 = (bf16[8,64,512]{2,1,0:T(8,128)(2,1)}, bf16[8,64,512]{2,1,0:T(8,128)(2,1)S(1)}, u32[]{:S(2)}, u32[]{:S(2)}) collective-permute-start(bf16[8,64,512]{2,1,0:T(8,128)(2,1)} %get-tuple-element.59), channel_id=1, source_target_pairs={{0,96},{32,0},{64,32},{96,64},{1,97},{33,1},{65,33},{97,65},{2,98}... | collective-permute-start | bytes 1572872 | tf_op jit(solution)/shard_map/ppermute | solution.py:418
  26.9 4.3 %collective-permute-done.4.mixed_up_ref = bf16[24,64,128]{2,1,0:T(8,128)(2,1)S(1)} collective-permute-done((bf16[24,64,128]{2,1,0:T(8,128)(2,1)S(1)}, bf16[24,64,128]{2,1,0:T(8,128)(2,1)S(1)}, u32[]{:S(2)}, u32[]{:S(2)}) %collective-permute-start.4) | collective-permute-done | bytes 393248 | tf_op jit(solution)/shard_map/ppermute | solution.py:418
  31.2 0.0 collective-permute-done.5.mixed_down_ref
  31.2 0.0 copy-done.5
  31.2 1.6 add_last_and_pick.2
  32.8 6.8 %all-to-all-start = ((bf16[16,2,64,256]{3,2,1,0:T(8,128)(2,1)}), bf16[16,2,64,256]{3,2,1,0:T(8,128)(2,1)}, u32[]{:S(2)}, u32[]{:S(2)}) async-start(bf16[16,2,64,256]{3,2,1,0:T(8,128)(2,1)} %add_last_and_pick.2), calls=%async_computation | async-start | bytes 2097152 | tf_op jit(solution)/shard_map/all_to_all | solution.py:436
  39.6 2.8 %collective-permute-done.6.up_ref = bf16[8,64,512]{2,1,0:T(8,128)(2,1)S(1)} collective-permute-done((bf16[8,64,512]{2,1,0:T(8,128)(2,1)}, bf16[8,64,512]{2,1,0:T(8,128)(2,1)S(1)}, u32[]{:S(2)}, u32[]{:S(2)}) %collective-permute-start.6) | collective-permute-done | bytes 524320 | tf_op jit(solution)/shard_map/ppermute | solution.py:418
  42.4 0.0 collective-permute-done.7.down_ref
  42.4 0.0 copy-start.6
  42.4 0.2 add_waiting.1
  42.6 0.1 collective-permute-start.8
  42.7 2.7 %collective-permute-start.9 = (bf16[4,64,768]{2,1,0:T(8,128)(2,1)S(1)}, bf16[4,64,768]{2,1,0:T(8,128)(2,1)S(1)}, u32[]{:S(2)}, u32[]{:S(2)}) collective-permute-start(bf16[4,64,768]{2,1,0:T(8,128)(2,1)S(1)} %get-tuple-element.64), channel_id=1, source_target_pairs={{0,96},{32,0},{64,32},{96,64},{1,97},{33,1},{65,33},{97,65},{2,98}... | collective-permute-start | bytes 1179656 | tf_op jit(solution)/shard_map/ppermute | solution.py:418
  45.4 7.3 %collective-permute-done.8.late_up_ref = bf16[4,64,768]{2,1,0:T(8,128)(2,1)S(1)} collective-permute-done((bf16[4,64,768]{2,1,0:T(8,128)(2,1)S(1)}, bf16[4,64,768]{2,1,0:T(8,128)(2,1)S(1)}, u32[]{:S(2)}, u32[]{:S(2)}) %collective-permute-start.8) | collective-permute-done | bytes 393248 | tf_op jit(solution)/shard_map/ppermute | solution.py:418
  52.7 0.0 collective-permute-done.9.late_down_ref
  52.7 0.0 copy-done.6
  52.7 2.5 %add_last_and_pick.3 = bf16[16,2,64,768]{3,2,1,0:T(8,128)(2,1)} custom-call(s32[2,128]{1,0:T(2,128)S(1)} %bitcast.12, bf16[8,64,256]{2,1,0:T(8,128)(2,1)S(1)} %get-tuple-element.52.b_ref, bf16[24,64,128]{2,1,0:T(8,128)(2,1)S(1)} %collective-permute-done.4.mixed_up_ref, bf16[24,64,128]{2,1,0:T(8,128)(2,1)S(1)} %collective-permute-done.5.mixed_down_ref, ...), custom_call_target="tpu_custom_call" | custom-call | bytes 5505024 | tf_op jit(solution)/shard_map/add_last_and_pick/pallas_call | solution.py:201
  55.2 0.0 all-to-all-done.grad_ref.refs_0_
  55.2 6.7 %all-to-all-start.1 = ((bf16[16,2,64,768]{3,2,1,0:T(8,128)(2,1)}), bf16[16,2,64,768]{3,2,1,0:T(8,128)(2,1)S(1)}, u32[]{:S(2)}, u32[]{:S(2)}) async-start(bf16[16,2,64,768]{3,2,1,0:T(8,128)(2,1)} %add_last_and_pick.3), calls=%async_computation.1 | async-start | bytes 6291456 | tf_op jit(solution)/shard_map/all_to_all | solution.py:439
  61.9 0.0 copy-start
  61.9 2.2 %copy-done = bf16[1,2,1024,1024]{3,2,1,0:T(8,128)(2,1)S(1)} copy-done((bf16[1,2,1024,1024]{3,2,1,0:T(8,128)(2,1)S(1)}, bf16[1,2,1024,1024]{3,2,1,0:T(8,128)(2,1)}, u32[]{:S(2)}) %copy-start) | copy-done | bytes 4194328
  64.1 2.5 %left_product.1.part_ref = bf16[2,1024,256]{2,1,0:T(8,128)(2,1)S(1)} custom-call(bf16[2,1024,1024]{2,1,0:T(8,128)(2,1)S(1)} %bitcast.9, bf16[16,2,64,256]{3,2,1,0:T(8,128)(2,1)} %all-to-all-done.grad_ref.refs_0_), custom_call_target="tpu_custom_call" | custom-call | flops 1073741824 | bytes 6291456 | tf_op jit(solution)/shard_map/left_product/pallas_call | solution.py:258
  66.6 0.0 copy-start.3
  66.6 1.0 copy-done.3
  67.6 33.5 %all-to-all-done.1.grad_ref.refs_1_ = bf16[16,2,64,768]{3,2,1,0:T(8,128)(2,1)S(1)} async-done(((bf16[16,2,64,768]{3,2,1,0:T(8,128)(2,1)}), bf16[16,2,64,768]{3,2,1,0:T(8,128)(2,1)S(1)}, u32[]{:S(2)}, u32[]{:S(2)}) %all-to-all-start.1) | async-done | bytes 3145760 | tf_op jit(solution)/shard_map/all_to_all | solution.py:439
  101.1 0.0 copy-start.1
  101.1 1.7 copy-done.1
  102.7 12.6 %finish_update.1 = bf16[8,16,2,64,128]{4,3,2,1,0:T(8,128)(2,1)} custom-call(bf16[2,1024,1024]{2,1,0:T(8,128)(2,1)} %bitcast.8, bf16[2,1024,1024]{2,1,0:T(8,128)(2,1)} %bitcast.17, bf16[2,1024,256]{2,1,0:T(8,128)(2,1)} %copy-done.3, bf16[16,2,64,768]{3,2,1,0:T(8,128)(2,1)} %copy-done.1), custom_call_target="tpu_custom_call" | custom-call | flops 7516192768 | bytes 12582912 | tf_op jit(solution)/shard_map/finish_update/pallas_call | solution.py:317
  115.3 0.0 copy-start.2
  115.3 10.2 %all-to-all-start.2 = ((bf16[128,2,64,128]{3,2,1,0:T(8,128)(2,1)}), bf16[128,2,64,128]{3,2,1,0:T(8,128)(2,1)}, u32[]{:S(2)}, u32[]{:S(2)}) async-start(bf16[128,2,64,128]{3,2,1,0:T(8,128)(2,1)} %bitcast.16), calls=%async_computation.2 | async-start | bytes 8388608 | tf_op jit(solution)/shard_map/all_to_all | solution.py:445
  125.5 0.0 copy-done.2
  125.5 13.8 %gram_products.1 = (bf16[2,1024,1024]{2,1,0:T(8,128)(2,1)}, bf16[2,1024,1024]{2,1,0:T(8,128)(2,1)}, s32[65]{0:T(128)S(1)}) custom-call(s32[2,128]{1,0:T(2,128)S(1)} %bitcast.13, bf16[16,2,64,256]{3,2,1,0:T(8,128)(2,1)} %all-to-all-done.grad_ref.refs_0_, bf16[16,2,64,768]{3,2,1,0:T(8,128)(2,1)S(1)} %copy-done.2), custom_call_target="tpu_custom_call" | custom-call | flops 8589934592 | bytes 12582912 | tf_op jit(solution)/shard_map/gram_products/pallas_call | solution.py:372
  139.3 0.0 copy-start.7
  139.3 0.5 copy-done.7
  139.8 37.2 %all-to-all-done.2 = bf16[128,2,64,128]{3,2,1,0:T(8,128)(2,1)} async-done(((bf16[128,2,64,128]{3,2,1,0:T(8,128)(2,1)}), bf16[128,2,64,128]{3,2,1,0:T(8,128)(2,1)}, u32[]{:S(2)}, u32[]{:S(2)}) %all-to-all-start.2) | async-done | bytes 4194336 | tf_op jit(solution)/shard_map/all_to_all | solution.py:445
  177.1 2.8 %collect_update.1 = bf16[64,64,128]{2,1,0:T(8,128)(2,1)} custom-call(s32[65]{0:T(128)} %copy-done.7, bf16[256,64,128]{2,1,0:T(8,128)(2,1)} %bitcast.7.got_ref), custom_call_target="tpu_custom_call" | custom-call | bytes 4194304 | tf_op jit(solution)/shard_map/collect_update/pallas_call | solution.py:394
Async XLA Ops:
  0.6 0.7 copy-start.4
  4.2 5.3 %collective-permute-start = (bf16[32,64,256]{2,1,0:T(8,128)(2,1)S(1)}, bf16[32,64,256]{2,1,0:T(8,128)(2,1)S(1)}, u32[]{:S(2)}, u32[]{:S(2)}) collective-permute-start(bf16[32,64,256]{2,1,0:T(8,128)(2,1)S(1)} %get-tuple-element.39), channel_id=1, source_target_pairs={{0,16},{16,0},{1,17},{17,1},{2,18},{18,2},{3,19},{19,3},{4,20},{20... | collective-permute-start | bytes 3145736 | tf_op jit(solution)/shard_map/ppermute | solution.py:421
  9.5 10.5 %collective-permute-start.3 = (bf16[32,64,768]{2,1,0:T(8,128)(2,1)S(1)}, bf16[32,64,768]{2,1,0:T(8,128)(2,1)S(1)}, u32[]{:S(2)}, u32[]{:S(2)}) collective-permute-start(bf16[32,64,768]{2,1,0:T(8,128)(2,1)S(1)} %get-tuple-element.51), channel_id=1, source_target_pairs={{0,16},{16,0},{1,17},{17,1},{2,18},{18,2},{3,19},{19,3},{4,20},{20... | collective-permute-start | bytes 9437192 | tf_op jit(solution)/shard_map/ppermute | solution.py:424
  9.9 10.2 %collective-permute-start.1 = (bf16[8,64,256]{2,1,0:T(8,128)(2,1)S(1)}, bf16[8,64,256]{2,1,0:T(8,128)(2,1)S(1)}, u32[]{:S(2)}, u32[]{:S(2)}) collective-permute-start(bf16[8,64,256]{2,1,0:T(8,128)(2,1)S(1)} %get-tuple-element.48), channel_id=1, source_target_pairs={{0,32},{32,64},{64,96},{96,0},{1,33},{33,65},{65,97},{97,1},{2,34}... | collective-permute-start | bytes 786440 | tf_op jit(solution)/shard_map/ppermute | solution.py:418
  11.6 8.4 %collective-permute-start.2 = (bf16[8,64,256]{2,1,0:T(8,128)(2,1)S(1)}, bf16[8,64,256]{2,1,0:T(8,128)(2,1)S(1)}, u32[]{:S(2)}, u32[]{:S(2)}) collective-permute-start(bf16[8,64,256]{2,1,0:T(8,128)(2,1)S(1)} %get-tuple-element.49), channel_id=1, source_target_pairs={{0,96},{32,0},{64,32},{96,64},{1,97},{33,1},{65,33},{97,65},{2,98}... | collective-permute-start | bytes 786440 | tf_op jit(solution)/shard_map/ppermute | solution.py:418
  20.0 11.2 %copy-start.5 = (s32[128,2]{0,1:T(2,128)S(1)}, s32[128,2]{0,1:T(2,128)}, u32[]{:S(2)}) copy-start(s32[128,2]{0,1:T(2,128)} %param.5) | copy-start | bytes 3076
  20.3 10.9 %collective-permute-start.4 = (bf16[24,64,128]{2,1,0:T(8,128)(2,1)S(1)}, bf16[24,64,128]{2,1,0:T(8,128)(2,1)S(1)}, u32[]{:S(2)}, u32[]{:S(2)}) collective-permute-start(bf16[24,64,128]{2,1,0:T(8,128)(2,1)S(1)} %get-tuple-element.56), channel_id=1, source_target_pairs={{0,32},{32,64},{64,96},{96,0},{1,33},{33,65},{65,97},{97,1},{2,34}... | collective-permute-start | bytes 1179656 | tf_op jit(solution)/shard_map/ppermute | solution.py:418
  20.7 10.5 %collective-permute-start.5 = (bf16[24,64,128]{2,1,0:T(8,128)(2,1)S(1)}, bf16[24,64,128]{2,1,0:T(8,128)(2,1)S(1)}, u32[]{:S(2)}, u32[]{:S(2)}) collective-permute-start(bf16[24,64,128]{2,1,0:T(8,128)(2,1)S(1)} %get-tuple-element.57), channel_id=1, source_target_pairs={{0,96},{32,0},{64,32},{96,64},{1,97},{33,1},{65,33},{97,65},{2,98}... | collective-permute-start | bytes 1179656 | tf_op jit(solution)/shard_map/ppermute | solution.py:418
  24.2 18.3 %collective-permute-start.6 = (bf16[8,64,512]{2,1,0:T(8,128)(2,1)}, bf16[8,64,512]{2,1,0:T(8,128)(2,1)S(1)}, u32[]{:S(2)}, u32[]{:S(2)}) collective-permute-start(bf16[8,64,512]{2,1,0:T(8,128)(2,1)} %get-tuple-element.58), channel_id=1, source_target_pairs={{0,32},{32,64},{64,96},{96,0},{1,33},{33,65},{65,97},{97,1},{2,34}... | collective-permute-start | bytes 1572872 | tf_op jit(solution)/shard_map/ppermute | solution.py:418
  24.2 18.3 %collective-permute-start.7 = (bf16[8,64,512]{2,1,0:T(8,128)(2,1)}, bf16[8,64,512]{2,1,0:T(8,128)(2,1)S(1)}, u32[]{:S(2)}, u32[]{:S(2)}) collective-permute-start(bf16[8,64,512]{2,1,0:T(8,128)(2,1)} %get-tuple-element.59), channel_id=1, source_target_pairs={{0,96},{32,0},{64,32},{96,64},{1,97},{33,1},{65,33},{97,65},{2,98}... | collective-permute-start | bytes 1572872 | tf_op jit(solution)/shard_map/ppermute | solution.py:418
  32.8 22.4 %all-to-all-start = ((bf16[16,2,64,256]{3,2,1,0:T(8,128)(2,1)}), bf16[16,2,64,256]{3,2,1,0:T(8,128)(2,1)}, u32[]{:S(2)}, u32[]{:S(2)}) async-start(bf16[16,2,64,256]{3,2,1,0:T(8,128)(2,1)} %add_last_and_pick.2), calls=%async_computation | async-start | bytes 2097152 | tf_op jit(solution)/shard_map/all_to_all | solution.py:436
  42.4 10.3 %copy-start.6 = (s32[128,2]{0,1:T(2,128)S(1)}, s32[128,2]{0,1:T(2,128)}, u32[]{:S(2)}) copy-start(s32[128,2]{0,1:T(2,128)} %param.5) | copy-start | bytes 3076
  42.6 10.1 %collective-permute-start.8 = (bf16[4,64,768]{2,1,0:T(8,128)(2,1)S(1)}, bf16[4,64,768]{2,1,0:T(8,128)(2,1)S(1)}, u32[]{:S(2)}, u32[]{:S(2)}) collective-permute-start(bf16[4,64,768]{2,1,0:T(8,128)(2,1)S(1)} %get-tuple-element.63), channel_id=1, source_target_pairs={{0,32},{32,64},{64,96},{96,0},{1,33},{33,65},{65,97},{97,1},{2,34}... | collective-permute-start | bytes 1179656 | tf_op jit(solution)/shard_map/ppermute | solution.py:418
  42.7 10.0 %collective-permute-start.9 = (bf16[4,64,768]{2,1,0:T(8,128)(2,1)S(1)}, bf16[4,64,768]{2,1,0:T(8,128)(2,1)S(1)}, u32[]{:S(2)}, u32[]{:S(2)}) collective-permute-start(bf16[4,64,768]{2,1,0:T(8,128)(2,1)S(1)} %get-tuple-element.64), channel_id=1, source_target_pairs={{0,96},{32,0},{64,32},{96,64},{1,97},{33,1},{65,33},{97,65},{2,98}... | collective-permute-start | bytes 1179656 | tf_op jit(solution)/shard_map/ppermute | solution.py:418
  55.2 45.8 %all-to-all-start.1 = ((bf16[16,2,64,768]{3,2,1,0:T(8,128)(2,1)}), bf16[16,2,64,768]{3,2,1,0:T(8,128)(2,1)S(1)}, u32[]{:S(2)}, u32[]{:S(2)}) async-start(bf16[16,2,64,768]{3,2,1,0:T(8,128)(2,1)} %add_last_and_pick.3), calls=%async_computation.1 | async-start | bytes 6291456 | tf_op jit(solution)/shard_map/all_to_all | solution.py:439
  61.9 2.2 %copy-start = (bf16[1,2,1024,1024]{3,2,1,0:T(8,128)(2,1)S(1)}, bf16[1,2,1024,1024]{3,2,1,0:T(8,128)(2,1)}, u32[]{:S(2)}) copy-start(bf16[1,2,1024,1024]{3,2,1,0:T(8,128)(2,1)} %param.6) | copy-start | bytes 12582916
  66.6 1.0 copy-start.3
  101.1 1.7 copy-start.1
  115.3 10.2 %copy-start.2 = (bf16[16,2,64,768]{3,2,1,0:T(8,128)(2,1)S(1)}, bf16[16,2,64,768]{3,2,1,0:T(8,128)(2,1)}, u32[]{:S(2)}) copy-start(bf16[16,2,64,768]{3,2,1,0:T(8,128)(2,1)} %copy-done.1) | copy-start | bytes 9437188
  115.3 61.8 %all-to-all-start.2 = ((bf16[128,2,64,128]{3,2,1,0:T(8,128)(2,1)}), bf16[128,2,64,128]{3,2,1,0:T(8,128)(2,1)}, u32[]{:S(2)}, u32[]{:S(2)}) async-start(bf16[128,2,64,128]{3,2,1,0:T(8,128)(2,1)} %bitcast.16), calls=%async_computation.2 | async-start | bytes 8388608 | tf_op jit(solution)/shard_map/all_to_all | solution.py:445
  139.3 0.5 copy-start.7

commit v5 on v2

--- a/solution.py
+++ b/solution.py
@@ -290,19 +290,17 @@
                 copies[c, name] = pltpu.make_async_copy(*pairs[name], sems.at[len(copies)])
                 copies[c, name].start()
 
-        fetch(0, "left", "grad")
+        for c in range(slots):
+            fetch(c, "left", "grad", "part", "right")
         for c in range(slots):
             copies[c, "left"].wait()
             copies[c, "grad"].wait()
-            fetch(c, "part", "right")
             half[:, done:] = jnp.dot(
                 left[c], grad[c].reshape(size, width), preferred_element_type=F32
             ).astype(BF16)
             copies[c, "part"].wait()
             half[:, :done] = part[c]
             copies[c, "right"].wait()
-            if c + 1 < slots:
-                fetch(c + 1, "left", "grad")
             for n in range(size // tile):
                 total = jnp.dot(
                     half[...], right[c, :, n * tile : (n + 1) * tile], preferred_element_type=F32

time: 178 us -> 178 us (level)
  no operation moved by 1% of the time
where the time goes in v5:
time: 178 us
  waiting for transfers between devices  88.9 us (50%)
  Pallas kernels  44.4 us (25%)
  starting transfers between devices  37.6 us (21%)
  local copies, waits for them, and re-layouts  5.98 us (3%)
    all_to_all x1, waiting for transfers between devices, local(): lax.all_to_all(pieces, ('z', 'core', 'owner'), split_axis=0, concat_axis=...  37.2 us
    all_to_all x2, waiting for transfers between devices, local(): lax.all_to_all(picked, 'owner', split_axis=0, concat_axis=0, tiled=True)  32.7 us
    ppermute x8, waiting for transfers between devices, along_z(): return (lax.ppermute(pair[0], 'z', up), lax.ppermute(pair[1], 'z', down))  19 us
    pallas_call x1, Pallas kernels, gram_products(): pl.pallas_call(body, grid=(slots, size // tile), in_specs=[SMEM] + [pl.Bl...  13.8 us
    all_to_all x1, starting transfers between devices, local(): lax.all_to_all(pieces, ('z', 'core', 'owner'), split_axis=0, concat_axis=...  13.1 us
    pallas_call x1, Pallas kernels, finish_update(): pl.pallas_call(body, in_specs=[HBM] * 4, out_specs=HBM, out_shape=shape(s...  12.6 us
    ppermute x8, starting transfers between devices, along_z(): return (lax.ppermute(pair[0], 'z', up), lax.ppermute(pair[1], 'z', down))  12.2 us
    all_to_all x2, starting transfers between devices, local(): lax.all_to_all(picked, 'owner', split_axis=0, concat_axis=0, tiled=True)  10.8 us
  transfers between devices with their start and end apart: 13, of which 6 were waited for; matrix products, arithmetic and copies ran while one was open for 0% of the time, Pallas kernels for 14%

profile of v5, /device:TPU:1, one launch (start us, length us, event | category | flops | bytes accessed | tf_op | source)
XLA Modules:
  0.0 177.9 jit_solution(8350938353918942454)
XLA Ops:
  0.6 0.0 copy-start.4
  0.6 0.7 copy-done.4
  1.3 2.9 %gather_first.1 = (s32[72]{0:T(128)S(1)}, bf16[32,64,256]{2,1,0:T(8,128)(2,1)S(1)}) custom-call(s32[2,128]{1,0:T(2,128)S(1)} %bitcast.10, bf16[64,64,1024]{2,1,0:T(8,128)(2,1)} %bitcast.14), custom_call_target="tpu_custom_call" | custom-call | bytes 2097152 | tf_op jit(solution)/shard_map/gather_first/pallas_call | solution.py:77
  4.2 1.5 collective-permute-start
  5.7 3.8 %gather_rest.1 = (bf16[32,64,256]{2,1,0:T(8,128)(2,1)S(1)}, bf16[32,64,384]{2,1,0:T(8,128)(2,1)S(1)}, bf16[32,64,384]{2,1,0:T(8,128)(2,1)S(1)}, bf16[32,64,768]{2,1,0:T(8,128)(2,1)S(1)}) custom-call(s32[72]{0:T(128)S(1)} %get-tuple-element.37.block_ref, bf16[64,64,1024]{2,1,0:T(8,128)(2,1)} %bitcast.15), custom_call_target="tpu_custom_call" | custom-call | bytes 14680064 | tf_op jit(solution)/shard_map/gather_rest/pallas_call | solution.py:101
  9.5 0.0 collective-permute-done.got_ref
  9.5 0.1 collective-permute-start.3
  9.6 0.2 add_core_pair.2
  9.9 1.8 %collective-permute-start.1 = (bf16[8,64,256]{2,1,0:T(8,128)(2,1)S(1)}, bf16[8,64,256]{2,1,0:T(8,128)(2,1)S(1)}, u32[]{:S(2)}, u32[]{:S(2)}) collective-permute-start(bf16[8,64,256]{2,1,0:T(8,128)(2,1)S(1)} %get-tuple-element.48), channel_id=1, source_target_pairs={{0,32},{32,64},{64,96},{96,0},{1,33},{33,65},{65,97},{97,1},{2,34}... | collective-permute-start | bytes 786440 | tf_op jit(solution)/shard_map/ppermute | solution.py:415
  11.7 2.2 %collective-permute-start.2 = (bf16[8,64,256]{2,1,0:T(8,128)(2,1)S(1)}, bf16[8,64,256]{2,1,0:T(8,128)(2,1)S(1)}, u32[]{:S(2)}, u32[]{:S(2)}) collective-permute-start(bf16[8,64,256]{2,1,0:T(8,128)(2,1)S(1)} %get-tuple-element.49), channel_id=1, source_target_pairs={{0,96},{32,0},{64,32},{96,64},{1,97},{33,1},{65,33},{97,65},{2,98}... | collective-permute-start | bytes 786440 | tf_op jit(solution)/shard_map/ppermute | solution.py:415
  13.9 6.2 %collective-permute-done.1.up_ref = bf16[8,64,256]{2,1,0:T(8,128)(2,1)S(1)} collective-permute-done((bf16[8,64,256]{2,1,0:T(8,128)(2,1)S(1)}, bf16[8,64,256]{2,1,0:T(8,128)(2,1)S(1)}, u32[]{:S(2)}, u32[]{:S(2)}) %collective-permute-start.1) | collective-permute-done | bytes 262176 | tf_op jit(solution)/shard_map/ppermute | solution.py:415
  20.0 0.0 collective-permute-done.2.down_ref
  20.0 0.0 collective-permute-done.3.got_ref
  20.0 0.0 copy-start.5
  20.1 0.5 mix_first_second.1
  20.5 0.4 collective-permute-start.4
  20.9 2.3 %collective-permute-start.5 = (bf16[32,64,128]{2,1,0:T(8,128)(2,1)S(1)}, bf16[32,64,128]{2,1,0:T(8,128)(2,1)S(1)}, u32[]{:S(2)}, u32[]{:S(2)}) collective-permute-start(bf16[32,64,128]{2,1,0:T(8,128)(2,1)S(1)} %get-tuple-element.57), channel_id=1, source_target_pairs={{0,96},{32,0},{64,32},{96,64},{1,97},{33,1},{65,33},{97,65},{2,98}... | collective-permute-start | bytes 1572872 | tf_op jit(solution)/shard_map/ppermute | solution.py:415
  23.3 1.0 add_core_pair.3
  24.2 0.0 collective-permute-start.6
  24.2 2.7 %collective-permute-start.7 = (bf16[8,64,384]{2,1,0:T(8,128)(2,1)}, bf16[8,64,384]{2,1,0:T(8,128)(2,1)S(1)}, u32[]{:S(2)}, u32[]{:S(2)}) collective-permute-start(bf16[8,64,384]{2,1,0:T(8,128)(2,1)} %get-tuple-element.59), channel_id=1, source_target_pairs={{0,96},{32,0},{64,32},{96,64},{1,97},{33,1},{65,33},{97,65},{2,98}... | collective-permute-start | bytes 1179656 | tf_op jit(solution)/shard_map/ppermute | solution.py:415
  26.9 7.3 %collective-permute-done.4.mixed_up_ref = bf16[32,64,128]{2,1,0:T(8,128)(2,1)S(1)} collective-permute-done((bf16[32,64,128]{2,1,0:T(8,128)(2,1)S(1)}, bf16[32,64,128]{2,1,0:T(8,128)(2,1)S(1)}, u32[]{:S(2)}, u32[]{:S(2)}) %collective-permute-start.4) | collective-permute-done | bytes 524320 | tf_op jit(solution)/shard_map/ppermute | solution.py:415
  34.2 0.0 collective-permute-done.5.mixed_down_ref
  34.2 0.0 copy-done.5
  34.2 1.6 add_last_and_pick.2
  35.8 6.8 %all-to-all-start = ((bf16[16,2,64,256]{3,2,1,0:T(8,128)(2,1)}), bf16[16,2,64,256]{3,2,1,0:T(8,128)(2,1)}, u32[]{:S(2)}, u32[]{:S(2)}) async-start(bf16[16,2,64,256]{3,2,1,0:T(8,128)(2,1)} %add_last_and_pick.2), calls=%async_computation | async-start | bytes 2097152 | tf_op jit(solution)/shard_map/all_to_all | solution.py:433
  42.6 0.0 collective-permute-done.6.up_ref
  42.6 0.0 collective-permute-done.7.down_ref
  42.7 0.0 copy-start.6
  42.7 0.2 add_waiting.1
  42.9 0.1 collective-permute-start.8
  43.0 2.7 %collective-permute-start.9 = (bf16[4,64,768]{2,1,0:T(8,128)(2,1)S(1)}, bf16[4,64,768]{2,1,0:T(8,128)(2,1)S(1)}, u32[]{:S(2)}, u32[]{:S(2)}) collective-permute-start(bf16[4,64,768]{2,1,0:T(8,128)(2,1)S(1)} %get-tuple-element.64), channel_id=1, source_target_pairs={{0,96},{32,0},{64,32},{96,64},{1,97},{33,1},{65,33},{97,65},{2,98}... | collective-permute-start | bytes 1179656 | tf_op jit(solution)/shard_map/ppermute | solution.py:415
  45.6 5.6 %collective-permute-done.8.late_up_ref = bf16[4,64,768]{2,1,0:T(8,128)(2,1)S(1)} collective-permute-done((bf16[4,64,768]{2,1,0:T(8,128)(2,1)S(1)}, bf16[4,64,768]{2,1,0:T(8,128)(2,1)S(1)}, u32[]{:S(2)}, u32[]{:S(2)}) %collective-permute-start.8) | collective-permute-done | bytes 393248 | tf_op jit(solution)/shard_map/ppermute | solution.py:415
  51.2 0.0 collective-permute-done.9.late_down_ref
  51.2 0.0 copy-done.6
  51.2 2.5 %add_last_and_pick.3 = bf16[16,2,64,768]{3,2,1,0:T(8,128)(2,1)} custom-call(s32[2,128]{1,0:T(2,128)S(1)} %bitcast.12, bf16[8,64,384]{2,1,0:T(8,128)(2,1)S(1)} %get-tuple-element.52.b_ref, bf16[32,64,128]{2,1,0:T(8,128)(2,1)S(1)} %collective-permute-done.4.mixed_up_ref, bf16[32,64,128]{2,1,0:T(8,128)(2,1)S(1)} %collective-permute-done.5.mixed_down_ref, ...), custom_call_target="tpu_custom_call" | custom-call | bytes 5505024 | tf_op jit(solution)/shard_map/add_last_and_pick/pallas_call | solution.py:201
  53.7 2.6 %all-to-all-done.grad_ref.refs_0_ = bf16[16,2,64,256]{3,2,1,0:T(8,128)(2,1)} async-done(((bf16[16,2,64,256]{3,2,1,0:T(8,128)(2,1)}), bf16[16,2,64,256]{3,2,1,0:T(8,128)(2,1)}, u32[]{:S(2)}, u32[]{:S(2)}) %all-to-all-start) | async-done | bytes 1048608 | tf_op jit(solution)/shard_map/all_to_all | solution.py:433
  56.3 4.0 %all-to-all-start.1 = ((bf16[16,2,64,768]{3,2,1,0:T(8,128)(2,1)}), bf16[16,2,64,768]{3,2,1,0:T(8,128)(2,1)S(1)}, u32[]{:S(2)}, u32[]{:S(2)}) async-start(bf16[16,2,64,768]{3,2,1,0:T(8,128)(2,1)} %add_last_and_pick.3), calls=%async_computation.1 | async-start | bytes 6291456 | tf_op jit(solution)/shard_map/all_to_all | solution.py:436
  60.3 0.0 copy-start
  60.3 2.2 %copy-done = bf16[1,2,1024,1024]{3,2,1,0:T(8,128)(2,1)S(1)} copy-done((bf16[1,2,1024,1024]{3,2,1,0:T(8,128)(2,1)S(1)}, bf16[1,2,1024,1024]{3,2,1,0:T(8,128)(2,1)}, u32[]{:S(2)}) %copy-start) | copy-done | bytes 4194328
  62.5 2.5 %left_product.1.part_ref = bf16[2,1024,256]{2,1,0:T(8,128)(2,1)S(1)} custom-call(bf16[2,1024,1024]{2,1,0:T(8,128)(2,1)S(1)} %bitcast.9, bf16[16,2,64,256]{3,2,1,0:T(8,128)(2,1)} %all-to-all-done.grad_ref.refs_0_), custom_call_target="tpu_custom_call" | custom-call | flops 1073741824 | bytes 6291456 | tf_op jit(solution)/shard_map/left_product/pallas_call | solution.py:257
  65.0 0.0 copy-start.3
  65.0 1.0 copy-done.3
  65.9 30.1 %all-to-all-done.1.grad_ref.refs_1_ = bf16[16,2,64,768]{3,2,1,0:T(8,128)(2,1)S(1)} async-done(((bf16[16,2,64,768]{3,2,1,0:T(8,128)(2,1)}), bf16[16,2,64,768]{3,2,1,0:T(8,128)(2,1)S(1)}, u32[]{:S(2)}, u32[]{:S(2)}) %all-to-all-start.1) | async-done | bytes 3145760 | tf_op jit(solution)/shard_map/all_to_all | solution.py:436
  96.1 0.0 copy-start.1
  96.1 1.7 copy-done.1
  97.7 12.6 %finish_update.1 = bf16[8,16,2,64,128]{4,3,2,1,0:T(8,128)(2,1)} custom-call(bf16[2,1024,1024]{2,1,0:T(8,128)(2,1)} %bitcast.8, bf16[2,1024,1024]{2,1,0:T(8,128)(2,1)} %bitcast.17, bf16[2,1024,256]{2,1,0:T(8,128)(2,1)} %copy-done.3, bf16[16,2,64,768]{3,2,1,0:T(8,128)(2,1)} %copy-done.1), custom_call_target="tpu_custom_call" | custom-call | flops 7516192768 | bytes 12582912 | tf_op jit(solution)/shard_map/finish_update/pallas_call | solution.py:314
  110.3 0.0 copy-start.2
  110.3 13.1 %all-to-all-start.2 = ((bf16[128,2,64,128]{3,2,1,0:T(8,128)(2,1)}), bf16[128,2,64,128]{3,2,1,0:T(8,128)(2,1)}, u32[]{:S(2)}, u32[]{:S(2)}) async-start(bf16[128,2,64,128]{3,2,1,0:T(8,128)(2,1)} %bitcast.16), calls=%async_computation.2 | async-start | bytes 8388608 | tf_op jit(solution)/shard_map/all_to_all | solution.py:442
  123.4 0.0 copy-done.2
  123.4 13.8 %gram_products.1 = (bf16[2,1024,1024]{2,1,0:T(8,128)(2,1)}, bf16[2,1024,1024]{2,1,0:T(8,128)(2,1)}, s32[65]{0:T(128)S(1)}) custom-call(s32[2,128]{1,0:T(2,128)S(1)} %bitcast.13, bf16[16,2,64,256]{3,2,1,0:T(8,128)(2,1)} %all-to-all-done.grad_ref.refs_0_, bf16[16,2,64,768]{3,2,1,0:T(8,128)(2,1)S(1)} %copy-done.2), custom_call_target="tpu_custom_call" | custom-call | flops 8589934592 | bytes 12582912 | tf_op jit(solution)/shard_map/gram_products/pallas_call | solution.py:369
  137.2 0.0 copy-start.7
  137.2 0.5 copy-done.7
  137.7 37.2 %all-to-all-done.2 = bf16[128,2,64,128]{3,2,1,0:T(8,128)(2,1)} async-done(((bf16[128,2,64,128]{3,2,1,0:T(8,128)(2,1)}), bf16[128,2,64,128]{3,2,1,0:T(8,128)(2,1)}, u32[]{:S(2)}, u32[]{:S(2)}) %all-to-all-start.2) | async-done | bytes 4194336 | tf_op jit(solution)/shard_map/all_to_all | solution.py:442
  174.9 2.8 %collect_update.1 = bf16[64,64,128]{2,1,0:T(8,128)(2,1)} custom-call(s32[65]{0:T(128)} %copy-done.7, bf16[256,64,128]{2,1,0:T(8,128)(2,1)} %bitcast.7.got_ref), custom_call_target="tpu_custom_call" | custom-call | bytes 4194304 | tf_op jit(solution)/shard_map/collect_update/pallas_call | solution.py:391
Async XLA Ops:
  0.6 0.7 copy-start.4
  4.2 5.4 %collective-permute-start = (bf16[32,64,256]{2,1,0:T(8,128)(2,1)S(1)}, bf16[32,64,256]{2,1,0:T(8,128)(2,1)S(1)}, u32[]{:S(2)}, u32[]{:S(2)}) collective-permute-start(bf16[32,64,256]{2,1,0:T(8,128)(2,1)S(1)} %get-tuple-element.39), channel_id=1, source_target_pairs={{0,16},{16,0},{1,17},{17,1},{2,18},{18,2},{3,19},{19,3},{4,20},{20... | collective-permute-start | bytes 3145736 | tf_op jit(solution)/shard_map/ppermute | solution.py:418
  9.5 10.5 %collective-permute-start.3 = (bf16[32,64,768]{2,1,0:T(8,128)(2,1)S(1)}, bf16[32,64,768]{2,1,0:T(8,128)(2,1)S(1)}, u32[]{:S(2)}, u32[]{:S(2)}) collective-permute-start(bf16[32,64,768]{2,1,0:T(8,128)(2,1)S(1)} %get-tuple-element.51), channel_id=1, source_target_pairs={{0,16},{16,0},{1,17},{17,1},{2,18},{18,2},{3,19},{19,3},{4,20},{20... | collective-permute-start | bytes 9437192 | tf_op jit(solution)/shard_map/ppermute | solution.py:421
  9.9 10.2 %collective-permute-start.1 = (bf16[8,64,256]{2,1,0:T(8,128)(2,1)S(1)}, bf16[8,64,256]{2,1,0:T(8,128)(2,1)S(1)}, u32[]{:S(2)}, u32[]{:S(2)}) collective-permute-start(bf16[8,64,256]{2,1,0:T(8,128)(2,1)S(1)} %get-tuple-element.48), channel_id=1, source_target_pairs={{0,32},{32,64},{64,96},{96,0},{1,33},{33,65},{65,97},{97,1},{2,34}... | collective-permute-start | bytes 786440 | tf_op jit(solution)/shard_map/ppermute | solution.py:415
  11.7 8.4 %collective-permute-start.2 = (bf16[8,64,256]{2,1,0:T(8,128)(2,1)S(1)}, bf16[8,64,256]{2,1,0:T(8,128)(2,1)S(1)}, u32[]{:S(2)}, u32[]{:S(2)}) collective-permute-start(bf16[8,64,256]{2,1,0:T(8,128)(2,1)S(1)} %get-tuple-element.49), channel_id=1, source_target_pairs={{0,96},{32,0},{64,32},{96,64},{1,97},{33,1},{65,33},{97,65},{2,98}... | collective-permute-start | bytes 786440 | tf_op jit(solution)/shard_map/ppermute | solution.py:415
  20.0 14.1 %copy-start.5 = (s32[128,2]{0,1:T(2,128)S(1)}, s32[128,2]{0,1:T(2,128)}, u32[]{:S(2)}) copy-start(s32[128,2]{0,1:T(2,128)} %param.5) | copy-start | bytes 3076
  20.5 13.7 %collective-permute-start.4 = (bf16[32,64,128]{2,1,0:T(8,128)(2,1)S(1)}, bf16[32,64,128]{2,1,0:T(8,128)(2,1)S(1)}, u32[]{:S(2)}, u32[]{:S(2)}) collective-permute-start(bf16[32,64,128]{2,1,0:T(8,128)(2,1)S(1)} %get-tuple-element.56), channel_id=1, source_target_pairs={{0,32},{32,64},{64,96},{96,0},{1,33},{33,65},{65,97},{97,1},{2,34}... | collective-permute-start | bytes 1572872 | tf_op jit(solution)/shard_map/ppermute | solution.py:415
  20.9 13.3 %collective-permute-start.5 = (bf16[32,64,128]{2,1,0:T(8,128)(2,1)S(1)}, bf16[32,64,128]{2,1,0:T(8,128)(2,1)S(1)}, u32[]{:S(2)}, u32[]{:S(2)}) collective-permute-start(bf16[32,64,128]{2,1,0:T(8,128)(2,1)S(1)} %get-tuple-element.57), channel_id=1, source_target_pairs={{0,96},{32,0},{64,32},{96,64},{1,97},{33,1},{65,33},{97,65},{2,98}... | collective-permute-start | bytes 1572872 | tf_op jit(solution)/shard_map/ppermute | solution.py:415
  24.2 18.4 %collective-permute-start.6 = (bf16[8,64,384]{2,1,0:T(8,128)(2,1)}, bf16[8,64,384]{2,1,0:T(8,128)(2,1)S(1)}, u32[]{:S(2)}, u32[]{:S(2)}) collective-permute-start(bf16[8,64,384]{2,1,0:T(8,128)(2,1)} %get-tuple-element.58), channel_id=1, source_target_pairs={{0,32},{32,64},{64,96},{96,0},{1,33},{33,65},{65,97},{97,1},{2,34}... | collective-permute-start | bytes 1179656 | tf_op jit(solution)/shard_map/ppermute | solution.py:415
  24.2 18.4 %collective-permute-start.7 = (bf16[8,64,384]{2,1,0:T(8,128)(2,1)}, bf16[8,64,384]{2,1,0:T(8,128)(2,1)S(1)}, u32[]{:S(2)}, u32[]{:S(2)}) collective-permute-start(bf16[8,64,384]{2,1,0:T(8,128)(2,1)} %get-tuple-element.59), channel_id=1, source_target_pairs={{0,96},{32,0},{64,32},{96,64},{1,97},{33,1},{65,33},{97,65},{2,98}... | collective-permute-start | bytes 1179656 | tf_op jit(solution)/shard_map/ppermute | solution.py:415
  35.8 20.5 %all-to-all-start = ((bf16[16,2,64,256]{3,2,1,0:T(8,128)(2,1)}), bf16[16,2,64,256]{3,2,1,0:T(8,128)(2,1)}, u32[]{:S(2)}, u32[]{:S(2)}) async-start(bf16[16,2,64,256]{3,2,1,0:T(8,128)(2,1)} %add_last_and_pick.2), calls=%async_computation | async-start | bytes 2097152 | tf_op jit(solution)/shard_map/all_to_all | solution.py:433
  42.7 8.5 %copy-start.6 = (s32[128,2]{0,1:T(2,128)S(1)}, s32[128,2]{0,1:T(2,128)}, u32[]{:S(2)}) copy-start(s32[128,2]{0,1:T(2,128)} %param.5) | copy-start | bytes 3076
  42.9 8.3 %collective-permute-start.8 = (bf16[4,64,768]{2,1,0:T(8,128)(2,1)S(1)}, bf16[4,64,768]{2,1,0:T(8,128)(2,1)S(1)}, u32[]{:S(2)}, u32[]{:S(2)}) collective-permute-start(bf16[4,64,768]{2,1,0:T(8,128)(2,1)S(1)} %get-tuple-element.63), channel_id=1, source_target_pairs={{0,32},{32,64},{64,96},{96,0},{1,33},{33,65},{65,97},{97,1},{2,34}... | collective-permute-start | bytes 1179656 | tf_op jit(solution)/shard_map/ppermute | solution.py:415
  43.0 8.2 %collective-permute-start.9 = (bf16[4,64,768]{2,1,0:T(8,128)(2,1)S(1)}, bf16[4,64,768]{2,1,0:T(8,128)(2,1)S(1)}, u32[]{:S(2)}, u32[]{:S(2)}) collective-permute-start(bf16[4,64,768]{2,1,0:T(8,128)(2,1)S(1)} %get-tuple-element.64), channel_id=1, source_target_pairs={{0,96},{32,0},{64,32},{96,64},{1,97},{33,1},{65,33},{97,65},{2,98}... | collective-permute-start | bytes 1179656 | tf_op jit(solution)/shard_map/ppermute | solution.py:415
  56.3 39.8 %all-to-all-start.1 = ((bf16[16,2,64,768]{3,2,1,0:T(8,128)(2,1)}), bf16[16,2,64,768]{3,2,1,0:T(8,128)(2,1)S(1)}, u32[]{:S(2)}, u32[]{:S(2)}) async-start(bf16[16,2,64,768]{3,2,1,0:T(8,128)(2,1)} %add_last_and_pick.3), calls=%async_computation.1 | async-start | bytes 6291456 | tf_op jit(solution)/shard_map/all_to_all | solution.py:436
  60.3 2.2 %copy-start = (bf16[1,2,1024,1024]{3,2,1,0:T(8,128)(2,1)S(1)}, bf16[1,2,1024,1024]{3,2,1,0:T(8,128)(2,1)}, u32[]{:S(2)}) copy-start(bf16[1,2,1024,1024]{3,2,1,0:T(8,128)(2,1)} %param.6) | copy-start | bytes 12582916
  65.0 1.0 copy-start.3
  96.1 1.7 copy-start.1
  110.3 13.1 %copy-start.2 = (bf16[16,2,64,768]{3,2,1,0:T(8,128)(2,1)S(1)}, bf16[16,2,64,768]{3,2,1,0:T(8,128)(2,1)}, u32[]{:S(2)}) copy-start(bf16[16,2,64,768]{3,2,1,0:T(8,128)(2,1)} %copy-done.1) | copy-start | bytes 9437188
  110.3 64.6 %all-to-all-start.2 = ((bf16[128,2,64,128]{3,2,1,0:T(8,128)(2,1)}), bf16[128,2,64,128]{3,2,1,0:T(8,128)(2,1)}, u32[]{:S(2)}, u32[]{:S(2)}) async-start(bf16[128,2,64,128]{3,2,1,0:T(8,128)(2,1)} %bitcast.16), calls=%async_computation.2 | async-start | bytes 8388608 | tf_op jit(solution)/shard_map/all_to_all | solution.py:442
  137.2 0.5 copy-start.7
